TPU v7x, 512 devices: a whole 4x8x8 slice. The times are simulated.
512 devices in a mesh: code: 128 (over y, z, core), tok: 4 (over x).
Axes of the slice: x: 4, y: 8, z: 8, core: 2. Of those that a mesh axis runs over, the one named last changes fastest.
Arguments:
- tokens: bfloat16 [4096, 256], P('tok'), may hold values from -125 to 125
- codebook: bfloat16 [262144, 256], P('code'), may hold values from -2 to 2
- cotangent: bfloat16 [4096, 256], P('tok'), may hold values from -6 to 6
- indices: int32 [4096], P('tok'), may hold values from 0 to 262143
Outputs:
- grad_tokens: float32 [4096, 256], P('tok')
- grad_codebook: float32 [262144, 256], P(('code', 'tok'))
All inputs are finite; a program needn't handle non-finite values.
Results may differ from a plain program's by a relative error of at most 0.0095.
Values may be sent and summed in bfloat16 or wider, within the bound.
A program may use at most 64 MiB of HBM per device.

v0:
```python
import jax
import jax.numpy as jnp
from jax import lax
from jax.sharding import PartitionSpec as P


def shards(tokens, codebook, cotangent, indices):
    rows = tokens.shape[0]
    codes = codebook.shape[0]
    block = min(512, rows)
    count = rows // block
    dims = (((1,), (1,)), ((), ()))

    def scores(index):
        latent = tokens[index * block : (index + 1) * block]
        grads = cotangent[index * block : (index + 1) * block]
        logits = lax.dot_general(latent, codebook, dims, preferred_element_type=jnp.float32)
        back = lax.dot_general(grads, codebook, dims, preferred_element_type=jnp.float32)
        return (latent, logits, back)

    tops, totals, weights = ([], [], [])
    for index in range(count):
        latent, logits, back = scores(index)
        local_top = jnp.max(logits, axis=1)
        expo = jnp.exp(logits - local_top[:, None])
        tops.append(local_top)
        totals.append(jnp.sum(expo, axis=1))
        weights.append(jnp.sum(expo * back, axis=1))
    local_top = jnp.concatenate(tops)
    local_total = jnp.concatenate(totals)
    local_weight = jnp.concatenate(weights)
    top = lax.pmax(local_top, "code")
    factor = jnp.exp(local_top - top)
    total, weighted = lax.psum((local_total * factor, local_weight * factor), "code")
    ratio = weighted / total
    code_terms = jnp.zeros((codes, codebook.shape[1]), jnp.float32)
    token_terms = []
    for index in range(count):
        latent, logits, back = scores(index)
        head = top[index * block : (index + 1) * block]
        denom = total[index * block : (index + 1) * block]
        mean_back = ratio[index * block : (index + 1) * block]
        probs = jnp.exp(logits - head[:, None]) / denom[:, None]
        dlogits = (probs * (back - mean_back[:, None])).astype(jnp.bfloat16)
        term = jnp.dot(dlogits, codebook, preferred_element_type=jnp.float32)
        token_terms.append(term)
        code_terms = code_terms + lax.dot_general(
            dlogits, latent, (((0,), (0,)), ((), ())), preferred_element_type=jnp.float32
        )
    grad_tokens = jnp.concatenate(token_terms, axis=0)
    grad_tokens = lax.psum(grad_tokens, "code")
    first_code = lax.axis_index("code") * codes
    local_index = indices - first_code
    inside = (local_index >= 0) & (local_index < codes)
    slots = jnp.where(inside, local_index, codes)
    direct = jax.ops.segment_sum(cotangent.astype(jnp.float32), slots, num_segments=codes + 1)[
        :codes
    ]
    grad_codebook = lax.psum_scatter(
        (code_terms + direct).astype(jnp.bfloat16), "tok", scatter_dimension=0, tiled=True
    ).astype(jnp.float32)
    return (grad_tokens, grad_codebook)


def solution(mesh):
    return jax.shard_map(
        shards,
        mesh=mesh,
        in_specs=(P("tok", None), P("code", None), P("tok", None), P("tok")),
        out_specs=(P("tok", None), P(("code", "tok"), None)),
        check_vma=False,
    )
```

profile of v0, /device:TPU:1, one launch (start us, length us, event | category | flops | bytes accessed | tf_op | source)
XLA Modules:
  0.0 760.3 jit_solution(4799946137234764219)
XLA Ops:
  8.0 0.0 copy-start
  8.0 0.0 copy-start.5
  8.0 0.0 copy-start.4
  8.0 0.0 reduce-scatter.2.cloned.1.call-start
  8.1 1.1 copy-done
  9.2 3.7 fusion.22
  12.9 0.0 copy-done.5
  12.9 2.7 fusion.21
  15.6 254.7 %pmax.7 = f32[1024]{0:T(1024)S(1)} all-reduce(f32[1024]{0:T(1024)S(1)} %pad_maximum_fusion.1), channel_id=1, replica_groups=mesh['code'=128,'tok'=4] {'code'}, use_global_device_ids=true, to_apply=%region_2.0 | all-reduce | flops 1024 | bytes 8192 | tf_op jit(solution)/shard_map/pmax | solution.py:32
  270.2 0.0 copy-done.4
  270.2 0.0 copy-start.1
  270.2 5.3 fusion
  275.6 0.0 copy-done.1
  275.6 3.1 fusion.1
  278.7 255.2 %all-reduce = (f32[1024]{0:T(1024)S(1)}, f32[1024]{0:T(1024)S(1)}) all-reduce(f32[1024]{0:T(1024)S(1)} %get-tuple-element.9, f32[1024]{0:T(1024)S(1)} %get-tuple-element.8), channel_id=1, replica_groups=mesh['code'=128,'tok'=4] {'code'}, use_global_device_ids=true, to_apply=%region_8.0 | all-reduce | flops 2048 | bytes 16384 | tf_op jit(solution)/shard_map/psum | solution.py:34
  534.0 0.0 copy-start.6
  534.0 8.4 %multiply_convert_fusion = (bf16[512,2048]{1,0:T(8,128)(2,1)}, bf16[512,2048]{1,0:T(8,128)(2,1)S(1)}) fusion(f32[512,2048]{1,0:T(8,128)} %get-tuple-element.18, f32[512,2048]{1,0:T(8,128)} %get-tuple-element.17, f32[512]{0:T(512)S(1)} %get-tuple-element.15, f32[512]{0:T(512)S(1)} %get-tuple-element.13, f32[512]{0:T(512)S(1)} %get-tuple-element.11, ...), kind=kLoop, calls=%fused_computation.1 | loop fusion | flops 10485760 | bytes 20983808 | tf_op jit(solution)/shard_map/convert_element_type | solution.py:44
  542.4 0.0 copy-start.2
  542.4 0.0 copy-start.7
  542.4 1.3 copy-done.2
  543.7 0.0 copy-done.6
  543.7 0.7 fusion.14
  544.5 0.0 copy-done.7
  544.5 9.5 %scatter_custom_fusion = f32[2049,256]{1,0:T(8,128)} fusion(s32[1024]{0:T(1024)S(1)} %and_select_fusion, f32[]{:T(128)} %constant.7.clone.1, bf16[1024,256]{1,0:T(8,128)(2,1)} %param.6), kind=kCustom, calls=%fused_computation.12 | custom fusion | flops 524288 | bytes 2622468 | tf_op jit(solution)/shard_map/scatter-add | solution.py:56
  554.0 4.1 fusion.3
  558.1 0.0 copy-start.3
  558.1 0.0 reduce-scatter.2.cloned.1.call-update
  558.1 0.0 all-reduce.3.cloned.1.call-start
  558.1 2.4 fusion.23
  560.6 0.0 copy-done.3
  560.6 0.7 fusion.24
  561.3 1.0 pad_maximum_fusion
  562.3 0.0 all-reduce.3.cloned.1.call-update
  562.4 16.5 %reduce-scatter.2.cloned.1.call-done = bf16[512,256]{1,0:T(8,128)(2,1)} async-done(((bf16[2048,256]{1,0:T(8,128)(2,1)}), bf16[512,256]{1,0:T(8,128)(2,1)}) %reduce-scatter.2.cloned.1.call-update) | async-done | bytes 262160 | tf_op jit(solution)/shard_map/reduce_scatter | solution.py:59
  578.9 1.8 convert_element_type.19
  580.7 169.9 %all-reduce.3.cloned.1.call-done = f32[1024,256]{1,0:T(8,128)} async-done(((f32[1024,256]{1,0:T(8,128)}), f32[1024,256]{1,0:T(8,128)}) %all-reduce.3.cloned.1.call-update) | async-done | bytes 1048592 | tf_op jit(solution)/shard_map/psum | solution.py:51
  750.6 2.3 copy.7
  (7 shorter events, 0.0 us)
Async XLA Ops:
  8.0 1.2 copy-start
  8.0 4.9 copy-start.5
  8.0 262.2 %copy-start.4 = (bf16[1024,256]{1,0:T(8,128)(2,1)S(1)}, bf16[1024,256]{1,0:T(8,128)(2,1)}, u32[]{:S(2)}) copy-start(bf16[1024,256]{1,0:T(8,128)(2,1)} %param.6) | copy-start | bytes 1572868
  8.0 570.9 %reduce-scatter.2.cloned.1.call-start = ((), (), s32[]{:S(2)}) async-start(), calls=%async_computation.2 | async-start | bytes 1310720 | tf_op jit(solution)/shard_map/reduce_scatter | solution.py:59
  270.2 5.3 copy-start.1
  534.0 9.7 %copy-start.6 = (bf16[1024,256]{1,0:T(8,128)(2,1)S(1)}, bf16[1024,256]{1,0:T(8,128)(2,1)}, u32[]{:S(2)}) copy-start(bf16[1024,256]{1,0:T(8,128)(2,1)} %param.4) | copy-start | bytes 1572868
  542.4 1.3 copy-start.2
  542.4 2.1 copy-start.7
  558.1 2.5 copy-start.3
  558.1 192.5 %all-reduce.3.cloned.1.call-start = ((), (), s32[]{:S(2)}) async-start(), calls=%async_computation.1 | async-start | bytes 2097152 | tf_op jit(solution)/shard_map/psum | solution.py:51
Sparse Core Ops, SparseCore 0:
  558.2 20.6 reduce-scatter.1
Sparse Core Ops, SparseCore 1:
  562.5 188.1 all-reduce.2
where the time goes:
time: 761 us; the launch traced here: 760 us
  blocking collectives  510 us (67%)
  waiting for transfers between devices  186 us (24%)
  matrix products  22.7 us (3%)
  other arithmetic  20.7 us (3%)
  between operations  15.6 us (2%)
    psum x1, blocking collectives, shards(): lax.psum((local_total * factor, local_weight * factor), 'code')  255 us
    pmax x1, blocking collectives, shards(): top = lax.pmax(local_top, 'code')  255 us
    psum x1, waiting for transfers between devices, shards(): grad_tokens = lax.psum(grad_tokens, 'code')  170 us
    reduce_scatter x1, waiting for transfers between devices, shards(): lax.psum_scatter((code_terms + direct).astype(jnp.bfloat16), 'tok', scatt...  16.5 us
  transfers between devices with their start and end apart: 2, of which 2 were waited for; matrix products, arithmetic and copies ran while one was open for 1% of the time, Pallas kernels for 0%

commit v1 on v0

v1 whole, which is shorter than its diff:
```python
import functools

import jax
import jax.numpy as jnp
from jax import lax
from jax.experimental import pallas as pl
from jax.experimental.pallas import tpu as pltpu
from jax.sharding import PartitionSpec as P

MESH = pl.DeviceIdType.MESH
F32 = jnp.float32
BF16 = jnp.bfloat16
NT = (((1,), (1,)), ((), ()))

RING = 8
TOK = 1024
HALF = TOK // 2
CODES = 2048
D = 256
TILE = 256
TILES = CODES // TILE
QUARTER = CODES // 4
ROWS = D // 2 // RING


def to_grid(row):
    return jnp.concatenate([row[:, 128 * i : 128 * (i + 1)] for i in range(HALF // 128)], axis=0)


def to_row(grid):
    return jnp.concatenate([grid[i : i + 1] for i in range(HALF // 128)], axis=1)


def combine(parts):
    top = functools.reduce(jnp.maximum, [p[0:4] for p in parts])
    total = jnp.zeros_like(top)
    weighted = jnp.zeros_like(top)
    for p in parts:
        factor = jnp.exp(p[0:4] - top)
        total = total + p[4:8] * factor
        weighted = weighted + p[8:12] * factor
    return top, total, weighted


def kernel(
    tok_ref,
    cot_ref,
    cb_ref,
    idx_ref,
    grad_tok_ref,
    grad_cb_ref,
    expo,
    back,
    direct,
    cbt,
    uv_own,
    uv_other,
    uv_acc,
    uv_send,
    uv_recv,
    stat_own,
    stat_other,
    stat_1,
    stat_2,
    sum_2,
    final,
    cb_send,
    cb_recv,
    core_send,
    core_recv,
    ring_send,
    ring_recv,
    x_send,
    x_recv,
):
    code = lax.axis_index("code")
    x = lax.axis_index("tok")
    y, z, core = code // 16, (code // 2) % 8, code % 2
    other = (code + 1 - 2 * core, x)
    x_size = 4

    def along(axis, k):
        if axis == "z":
            return (y * 16 + ((z + k) % RING) * 2 + core, x)
        return (((y + k) % RING) * 16 + z * 2 + core, x)

    first = (("z", z), ("y", y))
    second = (("y", y), ("z", z))

    barrier = pltpu.get_barrier_semaphore()

    def greet(k, carry):
        for axis in ("z", "y"):
            pl.semaphore_signal(barrier, inc=1, device_id=along(axis, k), device_id_type=MESH)
        return carry

    lax.fori_loop(1, RING, greet, 0)
    for k in range(1, x_size):
        pl.semaphore_signal(barrier, inc=1, device_id=(code, (x + k) % x_size), device_id_type=MESH)
    pl.semaphore_signal(barrier, inc=1, device_id=other, device_id_type=MESH)

    def ring_copy(buf, stage, half, axis, me, k, src=None):
        slot = (me + k) % RING
        return pltpu.make_async_remote_copy(
            src_ref=buf.at[half, me] if src is None else src.at[half, slot],
            dst_ref=buf.at[half, me],
            send_sem=ring_send.at[stage, half, slot],
            recv_sem=ring_recv.at[stage, half, me],
            device_id=along(axis, k),
            device_id_type=MESH,
        )

    def ring_arrival(buf, stage, half, axis, me, k):
        slot = (me + k) % RING
        return pltpu.make_async_remote_copy(
            src_ref=buf.at[half, slot],
            dst_ref=buf.at[half, slot],
            send_sem=ring_send.at[stage, half, slot],
            recv_sem=ring_recv.at[stage, half, slot],
            device_id=along(axis, k),
            device_id_type=MESH,
        )

    def ring_start(buf, stage, order, src=None):
        def step(k, carry):
            for half in range(2):
                ring_copy(buf, stage, half, *order[half], k, src).start()
            return carry

        lax.fori_loop(1, RING, step, 0)

    def ring_wait(buf, stage, order):
        def step(k, carry):
            for half in range(2):
                ring_arrival(buf, stage, half, *order[half], k).wait_recv()
            return carry

        lax.fori_loop(1, RING, step, 0)

    def ring_drain(buf, stage, order, src=None):
        def step(k, carry):
            for half in range(2):
                ring_copy(buf, stage, half, *order[half], k, src).wait_send()
            return carry

        lax.fori_loop(1, RING, step, 0)

    def core_copy(src, dst, index):
        return pltpu.make_async_remote_copy(
            src_ref=src,
            dst_ref=dst,
            send_sem=core_send.at[index],
            recv_sem=core_recv.at[index],
            device_id=other,
            device_id_type=MESH,
        )

    def fold(value, op):
        return op(value.reshape(TILE // 8, 8, TOK), axis=0)

    def pass_logits(i, top):
        rows = pl.ds(pl.multiple_of(i * TILE, TILE), TILE)
        logits = lax.dot_general(cb_ref[rows], tok_ref[...], NT, preferred_element_type=F32)
        expo[rows] = logits
        return jnp.maximum(top, fold(logits, jnp.max))

    top = lax.fori_loop(0, TILES, pass_logits, jnp.full((8, TOK), -jnp.inf, F32))
    top = jnp.max(top, axis=0, keepdims=True)

    def pass_back(i, carry):
        total, weighted = carry
        rows = pl.ds(pl.multiple_of(i * TILE, TILE), TILE)
        proj = lax.dot_general(cb_ref[rows], cot_ref[...], NT, preferred_element_type=F32)
        back[rows] = proj
        e = jnp.exp(expo[rows] - top)
        expo[rows] = e
        return total + fold(e, jnp.sum), weighted + fold(e * proj, jnp.sum)

    zero = jnp.zeros((8, TOK), F32)
    total, weighted = lax.fori_loop(0, TILES, pass_back, (zero, zero))
    total = jnp.sum(total, axis=0, keepdims=True)
    weighted = jnp.sum(weighted, axis=0, keepdims=True)

    for half in range(2):
        span = slice(half * HALF, (half + 1) * HALF)
        stat_own[half, 0:4] = to_grid(top[:, span])
        stat_own[half, 4:8] = to_grid(total[:, span])
        stat_own[half, 8:12] = to_grid(weighted[:, span])
    pl.semaphore_wait(barrier, 2 * (RING - 1) + x_size - 1 + 1)
    stat_copy = core_copy(stat_own, stat_other, 0)
    stat_copy.start()

    def pass_turn(i, carry):
        rows = pl.ds(pl.multiple_of(i * TILE, TILE), TILE)
        cbt[:, rows] = cb_ref[rows].astype(F32).T.astype(BF16)
        return carry

    lax.fori_loop(0, TILES, pass_turn, 0)
    stat_copy.wait()

    scale, mean = [], []
    for half in range(2):
        states = [jnp.where(core == 0, a, b) for a, b in ((stat_own[half], stat_other[half]), (stat_other[half], stat_own[half]))]
        pair_top, pair_total, pair_weighted = combine(states)
        me = first[half][1]
        stat_1[half, me, 0:4] = pair_top
        stat_1[half, me, 4:8] = pair_total
        stat_1[half, me, 8:12] = pair_weighted
        scale.append(to_row(jnp.exp(stat_own[half, 0:4] - pair_top)))
        mean.append(to_row(pair_weighted / pair_total))
    ring_start(stat_1, 0, first)

    scale = jnp.concatenate(scale, axis=1)
    mean = jnp.concatenate(mean, axis=1)
    uv_acc[...] = jnp.zeros_like(uv_acc)

    def pass_uv(i, carry):
        rows = pl.ds(pl.multiple_of(i * TILE, TILE), TILE)
        e = expo[rows] * scale
        codes = cbt[:, rows]
        u = (e * (back[rows] - mean)).astype(BF16)
        uv_acc[0] += jnp.dot(codes, u, preferred_element_type=F32)
        uv_acc[1] += jnp.dot(codes, e.astype(BF16), preferred_element_type=F32)
        return carry

    lax.fori_loop(0, TILES, pass_uv, 0)
    for c in range(2):
        for which in range(2):
            for half in range(2):
                uv_own[c, which, half] = uv_acc[which, c * 128 : (c + 1) * 128, half * HALF : (half + 1) * HALF].astype(BF16)
    uv_copy = core_copy(uv_own.at[1 - core], uv_other, 1)
    uv_copy.start()
    uv_copy.wait()
    for half in range(2):
        me = first[half][1]
        for which in range(2):
            both = uv_own[core, which, half].astype(F32) + uv_other[which, half].astype(F32)
            for k in range(RING):
                uv_send[half, k, which] = both[k * ROWS : (k + 1) * ROWS].astype(BF16)
        uv_recv[half, me] = uv_send[half, me]
    ring_start(uv_recv, 1, first, uv_send)

    ring_wait(stat_1, 0, first)
    for half in range(2):
        ring_top, ring_total, ring_weighted = combine([stat_1[half, j] for j in range(RING)])
        me = second[half][1]
        stat_2[half, me, 0:4] = ring_top
        stat_2[half, me, 4:8] = ring_total
        stat_2[half, me, 8:12] = ring_weighted
    ring_start(stat_2, 2, second)

    def pass_direct(i, carry):
        rows = pl.ds(pl.multiple_of(i * TILE, TILE), TILE)
        slot = idx_ref[...] - (code * CODES + i * TILE)
        hot = lax.broadcasted_iota(jnp.int32, (TILE, TOK), 0) == slot
        hot = jnp.where(hot, 1.0, 0.0).astype(BF16)
        direct[rows] = jnp.dot(hot, cot_ref[...], preferred_element_type=F32)
        return carry

    lax.fori_loop(0, TILES, pass_direct, 0)

    ring_wait(stat_2, 2, second)
    state = [combine([stat_2[half, j] for j in range(RING)]) for half in range(2)]
    ratio = [w / t for _, t, w in state]
    local_scale = jnp.concatenate(
        [to_row(jnp.exp(stat_own[half, 0:4] - state[half][0]) / state[half][1]) for half in range(2)], axis=1
    )
    ratio_row = jnp.concatenate([to_row(ratio[half]) for half in range(2)], axis=1)

    def x_copy(k):
        return pltpu.make_async_remote_copy(
            src_ref=cb_send.at[k],
            dst_ref=cb_recv.at[k],
            send_sem=x_send.at[k],
            recv_sem=x_recv.at[k],
            device_id=(code, (x + k) % x_size),
            device_id_type=MESH,
        )

    def code_rows(k):
        base = ((x + k) % x_size) * QUARTER

        def step(i, carry):
            rows = pl.ds(pl.multiple_of(base + i * TILE, TILE), TILE)
            grad = (expo[rows] * local_scale * (back[rows] - ratio_row)).astype(BF16)
            part = jnp.dot(grad, tok_ref[...], preferred_element_type=F32) + direct[rows]
            cb_send[k, pl.ds(pl.multiple_of(i * TILE, TILE), TILE)] = part.astype(BF16)
            return carry

        lax.fori_loop(0, QUARTER // TILE, step, 0)

    code_rows(2)
    x_copy(2).start()

    ring_wait(uv_recv, 1, first)
    for half in range(2):
        acc = jnp.zeros((ROWS, HALF), F32)
        for j in range(RING):
            peer = stat_1[half, j]
            factor = jnp.exp(peer[0:4] - state[half][0]) / state[half][1]
            shift = peer[8:12] / peer[4:8] - ratio[half]
            acc = acc + to_row(factor) * (
                uv_recv[half, j, 0].astype(F32) + to_row(shift) * uv_recv[half, j, 1].astype(F32)
            )
        sum_2[half, second[half][1]] = acc.astype(BF16)
    ring_start(sum_2, 3, second)

    code_rows(1)
    x_copy(1).start()
    code_rows(3)
    x_copy(3).start()
    code_rows(0)

    ring_wait(sum_2, 3, second)
    for half in range(2):
        acc = functools.reduce(jnp.add, [sum_2[half, j].astype(F32) for j in range(RING)])
        final[core, half, first[half][1]] = acc.astype(BF16)

    def final_copy(half, k):
        axis, me = first[half]
        slot = (me + k) % RING
        return pltpu.make_async_remote_copy(
            src_ref=final.at[core, half, me],
            dst_ref=final.at[core, half, me],
            send_sem=ring_send.at[4, half, slot],
            recv_sem=ring_recv.at[4, half, me],
            device_id=along(axis, k),
            device_id_type=MESH,
        )

    def final_arrival(half, k):
        axis, me = first[half]
        slot = (me + k) % RING
        return pltpu.make_async_remote_copy(
            src_ref=final.at[core, half, slot],
            dst_ref=final.at[core, half, slot],
            send_sem=ring_send.at[4, half, slot],
            recv_sem=ring_recv.at[4, half, slot],
            device_id=along(axis, k),
            device_id_type=MESH,
        )

    def final_forward(half, slot, whose):
        return core_copy(final.at[whose, half, slot], final.at[whose, half, slot], 2 + half * RING + slot)

    def final_start(k, carry):
        for half in range(2):
            final_copy(half, k).start()
        return carry

    lax.fori_loop(1, RING, final_start, 0)
    for half in range(2):
        final_forward(half, first[half][1], core).start()

    def final_pass(k, carry):
        for half in range(2):
            final_arrival(half, k).wait_recv()
            final_forward(half, (first[half][1] + k) % RING, core).start()
        return carry

    lax.fori_loop(1, RING, final_pass, 0)

    for k in range(1, x_size):
        x_copy(k).wait_recv()
    acc = cb_send[0].astype(F32)
    for k in range(1, x_size):
        acc = acc + cb_recv[k].astype(F32)
    grad_cb_ref[...] = acc

    def final_end(k, carry):
        for half in range(2):
            final_forward(half, k, 1 - core).wait_recv()
            final_forward(half, k, core).wait_send()
        return carry

    lax.fori_loop(0, RING, final_end, 0)
    for half in range(2):
        for c in range(2):
            block = jnp.concatenate([final[c, half, j].astype(F32) for j in range(RING)], axis=0)
            grad_tok_ref[half * HALF : (half + 1) * HALF, c * 128 : (c + 1) * 128] = block.T

    ring_drain(stat_1, 0, first)
    ring_drain(uv_recv, 1, first, uv_send)
    ring_drain(stat_2, 2, second)
    ring_drain(sum_2, 3, second)

    def final_drain(k, carry):
        for half in range(2):
            final_copy(half, k).wait_send()
        return carry

    lax.fori_loop(1, RING, final_drain, 0)
    for k in range(1, x_size):
        x_copy(k).wait_send()


def shards(tokens, codebook, cotangent, indices):
    vmem = pl.BlockSpec(memory_space=pltpu.VMEM)
    return pl.pallas_call(
        kernel,
        out_shape=(
            jax.ShapeDtypeStruct((TOK, D), F32),
            jax.ShapeDtypeStruct((QUARTER, D), F32),
        ),
        in_specs=[vmem] * 4,
        out_specs=(vmem, vmem),
        scratch_shapes=[
            pltpu.VMEM((CODES, TOK), F32),
            pltpu.VMEM((CODES, TOK), F32),
            pltpu.VMEM((CODES, D), F32),
            pltpu.VMEM((D, CODES), BF16),
            pltpu.VMEM((2, 2, 2, 128, HALF), BF16),
            pltpu.VMEM((2, 2, 128, HALF), BF16),
            pltpu.VMEM((2, D, TOK), F32),
            pltpu.VMEM((2, RING, 2, ROWS, HALF), BF16),
            pltpu.VMEM((2, RING, 2, ROWS, HALF), BF16),
            pltpu.VMEM((2, 12, 128), F32),
            pltpu.VMEM((2, 12, 128), F32),
            pltpu.VMEM((2, RING, 12, 128), F32),
            pltpu.VMEM((2, RING, 12, 128), F32),
            pltpu.VMEM((2, RING, ROWS, HALF), BF16),
            pltpu.VMEM((2, 2, RING, ROWS, HALF), BF16),
            pltpu.VMEM((4, QUARTER, D), BF16),
            pltpu.VMEM((4, QUARTER, D), BF16),
            pltpu.SemaphoreType.DMA((2 + 2 * RING,)),
            pltpu.SemaphoreType.DMA((2 + 2 * RING,)),
            pltpu.SemaphoreType.DMA((5, 2, RING)),
            pltpu.SemaphoreType.DMA((5, 2, RING)),
            pltpu.SemaphoreType.DMA((4,)),
            pltpu.SemaphoreType.DMA((4,)),
        ],
        compiler_params=pltpu.CompilerParams(
            collective_id=0, has_side_effects=True, vmem_limit_bytes=56 * 1024 * 1024
        ),
        name="quantizer_backward",
    )(tokens, cotangent, codebook, indices.reshape(1, TOK))


def solution(mesh):
    return jax.shard_map(
        shards,
        mesh=mesh,
        in_specs=(P("tok", None), P("code", None), P("tok", None), P("tok")),
        out_specs=(P("tok", None), P(("code", "tok"), None)),
        check_vma=False,
    )
```

time: 761 us -> 56.9 us (0.07)
  blocking collectives: 510 us -> 0 us
  waiting for transfers between devices: 186 us -> 0 us
  Pallas kernels: 0 us -> 52.9 us
  matrix products: 22.7 us -> 0 us
  other arithmetic: 20.7 us -> 0 us
  between operations: 15.6 us -> 0.65 us
    psum x1 -> x0, blocking collectives: 255 us -> none  [shards(): lax.psum((local_total * factor, local_weight * factor), 'code')]
    pmax x1 -> x0, blocking collectives: 255 us -> none  [shards(): top = lax.pmax(local_top, 'code')]
    psum x1 -> x0, waiting for transfers between devices: 170 us -> none  [shards(): grad_tokens = lax.psum(grad_tokens, 'code')]
    pallas_call x0 -> x1, Pallas kernels: none -> 52.9 us  [shards(): pl.pallas_call(kernel, out_shape=(jax.ShapeDtypeStruct((TOK, D), F32), ja...]
    dot_general x8 -> x0, matrix products: 22.7 us -> none  [the longest x2 8.45 us: scores(): lax.dot_general(grads, codebook, dims, preferred_element_type=jnp.float32)]
    reduce_scatter x1 -> x0, waiting for transfers between devices: 16.5 us -> none  [shards(): lax.psum_scatter((code_terms + direct).astype(jnp.bfloat16), 'tok', scatt...]
    convert_element_type x2 -> x0, other arithmetic: 10.2 us -> none  [the longest x1 8.4 us: shards(): dlogits = (probs * (back - mean_back[:, None])).astype(jnp.bfloat16)]
    scatter-add x1 -> x0, other arithmetic: 9.49 us -> none  [shards(): jax.ops.segment_sum(cotangent.astype(jnp.float32), slots, num_segments=co...]
  transfers between devices with their start and end apart: 2 -> 0, of which waited for: 2 -> 0; matrix products, arithmetic and copies ran while one was open for 1% -> 0% of each run, Pallas kernels for 0% -> 0%
where the time goes in v1:
time: 56.9 us; the launch traced here: 56.7 us
  Pallas kernels  52.9 us (93%)
  local copies, waits for them, and re-layouts  3.12 us (5%)
  between operations  0.65 us (1%)
    pallas_call x1, Pallas kernels, shards(): pl.pallas_call(kernel, out_shape=(jax.ShapeDtypeStruct((TOK, D), F32), ja...  52.9 us
    unnamed x4, local copies, waits for them, and re-layouts  3.12 us

profile of v1, /device:TPU:1, one launch (start us, length us, event | category | flops | bytes accessed | tf_op | source)
XLA Modules:
  0.0 56.7 jit_solution(15802083320459934455)
XLA Ops:
  0.6 52.9 %quantizer_backward.1 = (f32[1024,256]{1,0:T(8,128)}, f32[512,256]{1,0:T(8,128)}) custom-call(bf16[1024,256]{1,0:T(8,128)(2,1)} %tok_ref.1, bf16[1024,256]{1,0:T(8,128)(2,1)} %cot_ref.1, bf16[2048,256]{1,0:T(8,128)(2,1)} %cb_ref.1, s32[1,1024]{1,0:T(1,128)} %bitcast.1), custom_call_target="tpu_custom_call" | custom-call | tf_op jit(solution)/shard_map/quantizer_backward/pallas_call | solution.py:399
  53.6 0.0 copy-start
  53.6 2.3 %copy.8 = f32[1024,256]{1,0:T(8,128)} copy(f32[1024,256]{1,0:T(8,128)} %get-tuple-element.4) | data formatting | bytes 2097152
  55.9 0.0 copy-done
  55.9 0.8 %copy.9 = f32[512,256]{1,0:T(8,128)} copy(f32[512,256]{1,0:T(8,128)S(1)} %copy-done) | data formatting | bytes 1048576
Async XLA Ops:
  53.6 2.3 %copy-start = (f32[512,256]{1,0:T(8,128)S(1)}, f32[512,256]{1,0:T(8,128)}, u32[]{:S(2)}) copy-start(f32[512,256]{1,0:T(8,128)} %get-tuple-element.5) | copy-start | bytes 1572868

commit v2 on v1

--- a/solution.py
+++ b/solution.py
@@ -17,8 +17,7 @@
 HALF = TOK // 2
 CODES = 2048
 D = 256
-TILE = 256
-TILES = CODES // TILE
+VMEM_LIMIT = 44 * 1024 * 1024
 QUARTER = CODES // 4
 ROWS = D // 2 // RING
 
@@ -43,19 +42,23 @@
 
 
 def kernel(
+    tok_hbm,
+    cot_hbm,
+    cb_hbm,
+    idx_hbm,
+    grad_tok_ref,
+    grad_cb_ref,
     tok_ref,
     cot_ref,
     cb_ref,
     idx_ref,
-    grad_tok_ref,
-    grad_cb_ref,
+    load_sem,
     expo,
     back,
     direct,
     cbt,
     uv_own,
     uv_other,
-    uv_acc,
     uv_send,
     uv_recv,
     stat_own,
@@ -84,6 +87,15 @@
             return (y * 16 + ((z + k) % RING) * 2 + core, x)
         return (((y + k) % RING) * 16 + z * 2 + core, x)
 
+    loads = [
+        pltpu.make_async_copy(src, dst, load_sem.at[i])
+        for i, (src, dst) in enumerate(
+            ((cb_hbm, cb_ref), (tok_hbm, tok_ref), (cot_hbm, cot_ref), (idx_hbm, idx_ref))
+        )
+    ]
+    for load in loads:
+        load.start()
+
     first = (("z", z), ("y", y))
     second = (("y", y), ("z", z))
 
@@ -156,30 +168,19 @@
         )
 
     def fold(value, op):
-        return op(value.reshape(TILE // 8, 8, TOK), axis=0)
-
-    def pass_logits(i, top):
-        rows = pl.ds(pl.multiple_of(i * TILE, TILE), TILE)
-        logits = lax.dot_general(cb_ref[rows], tok_ref[...], NT, preferred_element_type=F32)
-        expo[rows] = logits
-        return jnp.maximum(top, fold(logits, jnp.max))
-
-    top = lax.fori_loop(0, TILES, pass_logits, jnp.full((8, TOK), -jnp.inf, F32))
-    top = jnp.max(top, axis=0, keepdims=True)
-
-    def pass_back(i, carry):
-        total, weighted = carry
-        rows = pl.ds(pl.multiple_of(i * TILE, TILE), TILE)
-        proj = lax.dot_general(cb_ref[rows], cot_ref[...], NT, preferred_element_type=F32)
-        back[rows] = proj
-        e = jnp.exp(expo[rows] - top)
-        expo[rows] = e
-        return total + fold(e, jnp.sum), weighted + fold(e * proj, jnp.sum)
-
-    zero = jnp.zeros((8, TOK), F32)
-    total, weighted = lax.fori_loop(0, TILES, pass_back, (zero, zero))
-    total = jnp.sum(total, axis=0, keepdims=True)
-    weighted = jnp.sum(weighted, axis=0, keepdims=True)
+        return op(value.reshape(CODES // 8, 8, TOK), axis=0)
+
+    loads[0].wait()
+    loads[1].wait()
+    logits = lax.dot_general(cb_ref[...], tok_ref[...], NT, preferred_element_type=F32)
+    expo[...] = logits
+    loads[2].wait()
+    back[...] = lax.dot_general(cb_ref[...], cot_ref[...], NT, preferred_element_type=F32)
+    top = jnp.max(fold(logits, jnp.max), axis=0, keepdims=True)
+    e = jnp.exp(expo[...] - top)
+    expo[...] = e
+    total = jnp.sum(fold(e, jnp.sum), axis=0, keepdims=True)
+    weighted = jnp.sum(fold(e * back[...], jnp.sum), axis=0, keepdims=True)
 
     for half in range(2):
         span = slice(half * HALF, (half + 1) * HALF)
@@ -190,12 +191,7 @@
     stat_copy = core_copy(stat_own, stat_other, 0)
     stat_copy.start()
 
-    def pass_turn(i, carry):
-        rows = pl.ds(pl.multiple_of(i * TILE, TILE), TILE)
-        cbt[:, rows] = cb_ref[rows].astype(F32).T.astype(BF16)
-        return carry
-
-    lax.fori_loop(0, TILES, pass_turn, 0)
+    cbt[...] = cb_ref[...].T
     stat_copy.wait()
 
     scale, mean = [], []
@@ -210,24 +206,14 @@
         mean.append(to_row(pair_weighted / pair_total))
     ring_start(stat_1, 0, first)
 
-    scale = jnp.concatenate(scale, axis=1)
-    mean = jnp.concatenate(mean, axis=1)
-    uv_acc[...] = jnp.zeros_like(uv_acc)
-
-    def pass_uv(i, carry):
-        rows = pl.ds(pl.multiple_of(i * TILE, TILE), TILE)
-        e = expo[rows] * scale
-        codes = cbt[:, rows]
-        u = (e * (back[rows] - mean)).astype(BF16)
-        uv_acc[0] += jnp.dot(codes, u, preferred_element_type=F32)
-        uv_acc[1] += jnp.dot(codes, e.astype(BF16), preferred_element_type=F32)
-        return carry
-
-    lax.fori_loop(0, TILES, pass_uv, 0)
-    for c in range(2):
-        for which in range(2):
-            for half in range(2):
-                uv_own[c, which, half] = uv_acc[which, c * 128 : (c + 1) * 128, half * HALF : (half + 1) * HALF].astype(BF16)
+    for half in range(2):
+        span = slice(half * HALF, (half + 1) * HALF)
+        e = expo[:, span] * scale[half]
+        u = (e * (back[:, span] - mean[half])).astype(BF16)
+        for which, weight in ((0, u), (1, e.astype(BF16))):
+            value = jnp.dot(cbt[...], weight, preferred_element_type=F32).astype(BF16)
+            for c in range(2):
+                uv_own[c, which, half] = value[c * 128 : (c + 1) * 128]
     uv_copy = core_copy(uv_own.at[1 - core], uv_other, 1)
     uv_copy.start()
     uv_copy.wait()
@@ -249,15 +235,10 @@
         stat_2[half, me, 8:12] = ring_weighted
     ring_start(stat_2, 2, second)
 
-    def pass_direct(i, carry):
-        rows = pl.ds(pl.multiple_of(i * TILE, TILE), TILE)
-        slot = idx_ref[...] - (code * CODES + i * TILE)
-        hot = lax.broadcasted_iota(jnp.int32, (TILE, TOK), 0) == slot
-        hot = jnp.where(hot, 1.0, 0.0).astype(BF16)
-        direct[rows] = jnp.dot(hot, cot_ref[...], preferred_element_type=F32)
-        return carry
-
-    lax.fori_loop(0, TILES, pass_direct, 0)
+    loads[3].wait()
+    hot = lax.broadcasted_iota(jnp.int32, (CODES, TOK), 0) == idx_ref[...] - code * CODES
+    hot = jnp.where(hot, 1.0, 0.0).astype(BF16)
+    direct[...] = jnp.dot(hot, cot_ref[...], preferred_element_type=F32)
 
     ring_wait(stat_2, 2, second)
     state = [combine([stat_2[half, j] for j in range(RING)]) for half in range(2)]
@@ -278,16 +259,10 @@
         )
 
     def code_rows(k):
-        base = ((x + k) % x_size) * QUARTER
-
-        def step(i, carry):
-            rows = pl.ds(pl.multiple_of(base + i * TILE, TILE), TILE)
-            grad = (expo[rows] * local_scale * (back[rows] - ratio_row)).astype(BF16)
-            part = jnp.dot(grad, tok_ref[...], preferred_element_type=F32) + direct[rows]
-            cb_send[k, pl.ds(pl.multiple_of(i * TILE, TILE), TILE)] = part.astype(BF16)
-            return carry
-
-        lax.fori_loop(0, QUARTER // TILE, step, 0)
+        rows = pl.ds(pl.multiple_of(((x + k) % x_size) * QUARTER, QUARTER), QUARTER)
+        grad = (expo[rows] * local_scale * (back[rows] - ratio_row)).astype(BF16)
+        part = jnp.dot(grad, tok_ref[...], preferred_element_type=F32) + direct[rows]
+        cb_send[k] = part.astype(BF16)
 
     code_rows(2)
     x_copy(2).start()
@@ -394,24 +369,41 @@
         x_copy(k).wait_send()
 
 
+def write(grad_tok_ref, grad_cb_ref, tok_out, cb_out, sems):
+    copies = [
+        pltpu.make_async_copy(grad_tok_ref, tok_out, sems.at[0]),
+        pltpu.make_async_copy(grad_cb_ref, cb_out, sems.at[1]),
+    ]
+    for copy in copies:
+        copy.start()
+    for copy in copies:
+        copy.wait()
+
+
 def shards(tokens, codebook, cotangent, indices):
     vmem = pl.BlockSpec(memory_space=pltpu.VMEM)
-    return pl.pallas_call(
+    hbm = pl.BlockSpec(memory_space=pltpu.HBM)
+    shapes = (
+        jax.ShapeDtypeStruct((TOK, D), F32),
+        jax.ShapeDtypeStruct((QUARTER, D), F32),
+    )
+    grads = pl.pallas_call(
         kernel,
-        out_shape=(
-            jax.ShapeDtypeStruct((TOK, D), F32),
-            jax.ShapeDtypeStruct((QUARTER, D), F32),
-        ),
-        in_specs=[vmem] * 4,
+        out_shape=shapes,
+        in_specs=[hbm] * 4,
         out_specs=(vmem, vmem),
         scratch_shapes=[
+            pltpu.VMEM((TOK, D), BF16),
+            pltpu.VMEM((TOK, D), BF16),
+            pltpu.VMEM((CODES, D), BF16),
+            pltpu.VMEM((1, TOK), jnp.int32),
+            pltpu.SemaphoreType.DMA((4,)),
             pltpu.VMEM((CODES, TOK), F32),
             pltpu.VMEM((CODES, TOK), F32),
             pltpu.VMEM((CODES, D), F32),
             pltpu.VMEM((D, CODES), BF16),
             pltpu.VMEM((2, 2, 2, 128, HALF), BF16),
             pltpu.VMEM((2, 2, 128, HALF), BF16),
-            pltpu.VMEM((2, D, TOK), F32),
             pltpu.VMEM((2, RING, 2, ROWS, HALF), BF16),
             pltpu.VMEM((2, RING, 2, ROWS, HALF), BF16),
             pltpu.VMEM((2, 12, 128), F32),
@@ -430,10 +422,19 @@
             pltpu.SemaphoreType.DMA((4,)),
         ],
         compiler_params=pltpu.CompilerParams(
-            collective_id=0, has_side_effects=True, vmem_limit_bytes=56 * 1024 * 1024
+            collective_id=0, has_side_effects=True, vmem_limit_bytes=VMEM_LIMIT
         ),
         name="quantizer_backward",
-    )(tokens, cotangent, codebook, indices.reshape(1, TOK))
+    )(*(pltpu.with_memory_space_constraint(a, pltpu.HBM) for a in (tokens, cotangent, codebook, indices.reshape(1, TOK))))
+    return pl.pallas_call(
+        write,
+        out_shape=shapes,
+        in_specs=[vmem, vmem],
+        out_specs=(hbm, hbm),
+        scratch_shapes=[pltpu.SemaphoreType.DMA((2,))],
+        compiler_params=pltpu.CompilerParams(vmem_limit_bytes=8 * 1024 * 1024),
+        name="write_out",
+    )(*grads)
 
 
 def solution(mesh):

time: 56.9 us -> 50.8 us (0.89)
  local copies, waits for them, and re-layouts: 3.12 us -> 0 us
  Pallas kernels: 52.9 us -> 50 us
    unnamed x4 -> x0, local copies, waits for them, and re-layouts: 3.12 us -> none
    pallas_call x1 -> x2, Pallas kernels: 52.9 us -> 50 us  [the longest x1 48.8 us: shards(): pl.pallas_call(kernel, out_shape=shapes, in_specs=[hbm] * 4, out_specs=(v...]
where the time goes in v2:
time: 50.8 us; the launch traced here: 50.6 us
  Pallas kernels  50 us (98%)
  between operations  0.64 us (1%)
    pallas_call x1, Pallas kernels, shards(): pl.pallas_call(kernel, out_shape=shapes, in_specs=[hbm] * 4, out_specs=(v...  48.8 us
    pallas_call x1, Pallas kernels, shards(): pl.pallas_call(write, out_shape=shapes, in_specs=[vmem, vmem], out_specs=...  1.16 us

profile of v2, /device:TPU:1, one launch (start us, length us, event | category | flops | bytes accessed | tf_op | source)
XLA Modules:
  0.0 50.6 jit_solution(5736809398954721326)
XLA Ops:
  0.6 48.8 %quantizer_backward.1 = (f32[1024,256]{1,0:T(8,128)S(1)}, f32[512,256]{1,0:T(8,128)S(1)}) custom-call(bf16[1024,256]{1,0:T(8,128)(2,1)} %tok_hbm.1, bf16[1024,256]{1,0:T(8,128)(2,1)} %cot_hbm.1, bf16[2048,256]{1,0:T(8,128)(2,1)} %cb_hbm.1, s32[1,1024]{1,0:T(1,128)} %bitcast.1), custom_call_target="tpu_custom_call" | custom-call | tf_op jit(solution)/shard_map/quantizer_backward/pallas_call | solution.py:390
  49.5 1.2 %write_out.1 = (f32[1024,256]{1,0:T(8,128)}, f32[512,256]{1,0:T(8,128)}) custom-call(f32[1024,256]{1,0:T(8,128)S(1)} %get-tuple-element.4.grad_tok_ref, f32[512,256]{1,0:T(8,128)S(1)} %get-tuple-element.5.grad_cb_ref), custom_call_target="tpu_custom_call" | custom-call | tf_op jit(solution)/shard_map/write_out/pallas_call | solution.py:429

commit v3 on v2

--- a/solution.py
+++ b/solution.py
@@ -13,6 +13,7 @@
 NT = (((1,), (1,)), ((), ()))
 
 RING = 8
+FAR_FIRST = (4, 3, 5, 2, 6, 1, 7)
 TOK = 1024
 HALF = TOK // 2
 CODES = 2048
@@ -69,6 +70,8 @@
     final,
     cb_send,
     cb_recv,
+    far_recv,
+    cb_own,
     core_send,
     core_recv,
     ring_send,
@@ -107,7 +110,7 @@
         return carry
 
     lax.fori_loop(1, RING, greet, 0)
-    for k in range(1, x_size):
+    for k in (1, x_size - 1):
         pl.semaphore_signal(barrier, inc=1, device_id=(code, (x + k) % x_size), device_id_type=MESH)
     pl.semaphore_signal(barrier, inc=1, device_id=other, device_id_type=MESH)
 
@@ -133,21 +136,15 @@
             device_id_type=MESH,
         )
 
-    def ring_start(buf, stage, order, src=None):
-        def step(k, carry):
-            for half in range(2):
+    def ring_start(buf, stage, order, src=None, halves=(0, 1)):
+        for k in FAR_FIRST:
+            for half in halves:
                 ring_copy(buf, stage, half, *order[half], k, src).start()
-            return carry
-
-        lax.fori_loop(1, RING, step, 0)
 
     def ring_wait(buf, stage, order):
-        def step(k, carry):
+        for k in reversed(FAR_FIRST):
             for half in range(2):
                 ring_arrival(buf, stage, half, *order[half], k).wait_recv()
-            return carry
-
-        lax.fori_loop(1, RING, step, 0)
 
     def ring_drain(buf, stage, order, src=None):
         def step(k, carry):
@@ -187,7 +184,7 @@
         stat_own[half, 0:4] = to_grid(top[:, span])
         stat_own[half, 4:8] = to_grid(total[:, span])
         stat_own[half, 8:12] = to_grid(weighted[:, span])
-    pl.semaphore_wait(barrier, 2 * (RING - 1) + x_size - 1 + 1)
+    pl.semaphore_wait(barrier, 2 * (RING - 1) + 2 + 1)
     stat_copy = core_copy(stat_own, stat_other, 0)
     stat_copy.start()
 
@@ -206,6 +203,8 @@
         mean.append(to_row(pair_weighted / pair_total))
     ring_start(stat_1, 0, first)
 
+    uv_copies = [core_copy(uv_own.at[half, 1 - core], uv_other.at[half], 1 + half) for half in range(2)]
+
     for half in range(2):
         span = slice(half * HALF, (half + 1) * HALF)
         e = expo[:, span] * scale[half]
@@ -213,18 +212,20 @@
         for which, weight in ((0, u), (1, e.astype(BF16))):
             value = jnp.dot(cbt[...], weight, preferred_element_type=F32).astype(BF16)
             for c in range(2):
-                uv_own[c, which, half] = value[c * 128 : (c + 1) * 128]
-    uv_copy = core_copy(uv_own.at[1 - core], uv_other, 1)
-    uv_copy.start()
-    uv_copy.wait()
-    for half in range(2):
+                uv_own[half, c, which] = value[c * 128 : (c + 1) * 128]
+        uv_copies[half].start()
+
+    def uv_ring(half):
+        uv_copies[half].wait()
         me = first[half][1]
         for which in range(2):
-            both = uv_own[core, which, half].astype(F32) + uv_other[which, half].astype(F32)
+            both = uv_own[half, core, which].astype(F32) + uv_other[half, which].astype(F32)
             for k in range(RING):
                 uv_send[half, k, which] = both[k * ROWS : (k + 1) * ROWS].astype(BF16)
         uv_recv[half, me] = uv_send[half, me]
-    ring_start(uv_recv, 1, first, uv_send)
+        ring_start(uv_recv, 1, first, uv_send, (half,))
+
+    uv_ring(0)
 
     ring_wait(stat_1, 0, first)
     for half in range(2):
@@ -234,6 +235,7 @@
         stat_2[half, me, 4:8] = ring_total
         stat_2[half, me, 8:12] = ring_weighted
     ring_start(stat_2, 2, second)
+    uv_ring(1)
 
     loads[3].wait()
     hot = lax.broadcasted_iota(jnp.int32, (CODES, TOK), 0) == idx_ref[...] - code * CODES
@@ -248,24 +250,34 @@
     )
     ratio_row = jnp.concatenate([to_row(ratio[half]) for half in range(2)], axis=1)
 
-    def x_copy(k):
-        return pltpu.make_async_remote_copy(
-            src_ref=cb_send.at[k],
-            dst_ref=cb_recv.at[k],
-            send_sem=x_send.at[k],
-            recv_sem=x_recv.at[k],
-            device_id=(code, (x + k) % x_size),
-            device_id_type=MESH,
-        )
+    low, high = pl.ds(0, QUARTER // 2), pl.ds(QUARTER // 2, QUARTER // 2)
+
+    def x_copy(src, dst, index, side):
+        return pltpu.make_async_remote_copy(
+            src_ref=src,
+            dst_ref=dst,
+            send_sem=x_send.at[index],
+            recv_sem=x_recv.at[index],
+            device_id=(code, (x + (1, x_size - 1)[side]) % x_size),
+            device_id_type=MESH,
+        )
+
+    far_copies = [x_copy(cb_send.at[2, part], far_recv.at[side], side, side) for side, part in ((0, low), (1, high))]
+    near_copies = [
+        x_copy(cb_send.at[side, part], cb_recv.at[side, part], 2 + side, side) for side, part in ((0, high), (1, low))
+    ]
+    sum_copies = [
+        x_copy(cb_send.at[side, part], cb_recv.at[side, part], 4 + side, side) for side, part in ((0, low), (1, high))
+    ]
 
     def code_rows(k):
         rows = pl.ds(pl.multiple_of(((x + k) % x_size) * QUARTER, QUARTER), QUARTER)
         grad = (expo[rows] * local_scale * (back[rows] - ratio_row)).astype(BF16)
-        part = jnp.dot(grad, tok_ref[...], preferred_element_type=F32) + direct[rows]
-        cb_send[k] = part.astype(BF16)
-
-    code_rows(2)
-    x_copy(2).start()
+        return jnp.dot(grad, tok_ref[...], preferred_element_type=F32) + direct[rows]
+
+    cb_send[2] = code_rows(2).astype(BF16)
+    for copy in far_copies:
+        copy.start()
 
     ring_wait(uv_recv, 1, first)
     for half in range(2):
@@ -280,11 +292,20 @@
         sum_2[half, second[half][1]] = acc.astype(BF16)
     ring_start(sum_2, 3, second)
 
-    code_rows(1)
-    x_copy(1).start()
-    code_rows(3)
-    x_copy(3).start()
-    code_rows(0)
+    mid = QUARTER // 2
+    part = code_rows(1)
+    cb_send[0, high] = part[mid:].astype(BF16)
+    near_copies[0].start()
+    cb_own[0] = part[:mid]
+    part = code_rows(3)
+    cb_send[1, low] = part[:mid].astype(BF16)
+    near_copies[1].start()
+    cb_own[1] = part[mid:]
+    for side, part in ((0, low), (1, high)):
+        far_copies[side].wait_recv()
+        cb_send[side, part] = (cb_own[side] + far_recv[side].astype(F32)).astype(BF16)
+        sum_copies[side].start()
+    grad_cb_ref[...] = code_rows(0)
 
     ring_wait(sum_2, 3, second)
     for half in range(2):
@@ -316,31 +337,21 @@
         )
 
     def final_forward(half, slot, whose):
-        return core_copy(final.at[whose, half, slot], final.at[whose, half, slot], 2 + half * RING + slot)
-
-    def final_start(k, carry):
+        return core_copy(final.at[whose, half, slot], final.at[whose, half, slot], 3 + half * RING + slot)
+
+    for k in FAR_FIRST:
         for half in range(2):
             final_copy(half, k).start()
-        return carry
-
-    lax.fori_loop(1, RING, final_start, 0)
     for half in range(2):
         final_forward(half, first[half][1], core).start()
-
-    def final_pass(k, carry):
+    for k in reversed(FAR_FIRST):
         for half in range(2):
             final_arrival(half, k).wait_recv()
             final_forward(half, (first[half][1] + k) % RING, core).start()
-        return carry
-
-    lax.fori_loop(1, RING, final_pass, 0)
-
-    for k in range(1, x_size):
-        x_copy(k).wait_recv()
-    acc = cb_send[0].astype(F32)
-    for k in range(1, x_size):
-        acc = acc + cb_recv[k].astype(F32)
-    grad_cb_ref[...] = acc
+
+    for copy in near_copies + sum_copies:
+        copy.wait_recv()
+    grad_cb_ref[...] += cb_recv[0].astype(F32) + cb_recv[1].astype(F32)
 
     def final_end(k, carry):
         for half in range(2):
@@ -365,8 +376,8 @@
         return carry
 
     lax.fori_loop(1, RING, final_drain, 0)
-    for k in range(1, x_size):
-        x_copy(k).wait_send()
+    for copy in far_copies + near_copies + sum_copies:
+        copy.wait_send()
 
 
 def write(grad_tok_ref, grad_cb_ref, tok_out, cb_out, sems):
@@ -412,14 +423,16 @@
             pltpu.VMEM((2, RING, 12, 128), F32),
             pltpu.VMEM((2, RING, ROWS, HALF), BF16),
             pltpu.VMEM((2, 2, RING, ROWS, HALF), BF16),
-            pltpu.VMEM((4, QUARTER, D), BF16),
-            pltpu.VMEM((4, QUARTER, D), BF16),
-            pltpu.SemaphoreType.DMA((2 + 2 * RING,)),
-            pltpu.SemaphoreType.DMA((2 + 2 * RING,)),
+            pltpu.VMEM((3, QUARTER, D), BF16),
+            pltpu.VMEM((2, QUARTER, D), BF16),
+            pltpu.VMEM((2, QUARTER // 2, D), BF16),
+            pltpu.VMEM((2, QUARTER // 2, D), F32),
+            pltpu.SemaphoreType.DMA((3 + 2 * RING,)),
+            pltpu.SemaphoreType.DMA((3 + 2 * RING,)),
             pltpu.SemaphoreType.DMA((5, 2, RING)),
             pltpu.SemaphoreType.DMA((5, 2, RING)),
-            pltpu.SemaphoreType.DMA((4,)),
-            pltpu.SemaphoreType.DMA((4,)),
+            pltpu.SemaphoreType.DMA((6,)),
+            pltpu.SemaphoreType.DMA((6,)),
         ],
         compiler_params=pltpu.CompilerParams(
             collective_id=0, has_side_effects=True, vmem_limit_bytes=VMEM_LIMIT

time: 50.8 us -> 50.3 us (level)
  no operation moved by 1% of the time
where the time goes in v3:
time: 50.3 us; the launch traced here: 50.2 us
  Pallas kernels  49.5 us (98%)
  between operations  0.64 us (1%)
    pallas_call x1, Pallas kernels, shards(): pl.pallas_call(kernel, out_shape=shapes, in_specs=[hbm] * 4, out_specs=(v...  48.4 us
    pallas_call x1, Pallas kernels, shards(): pl.pallas_call(write, out_shape=shapes, in_specs=[vmem, vmem], out_specs=...  1.16 us

profile of v3, /device:TPU:1, one launch (start us, length us, event | category | flops | bytes accessed | tf_op | source)
XLA Modules:
  0.0 50.2 jit_solution(9547334271385929746)
XLA Ops:
  0.6 48.4 %quantizer_backward.1 = (f32[1024,256]{1,0:T(8,128)S(1)}, f32[512,256]{1,0:T(8,128)S(1)}) custom-call(bf16[1024,256]{1,0:T(8,128)(2,1)} %tok_hbm.1, bf16[1024,256]{1,0:T(8,128)(2,1)} %cot_hbm.1, bf16[2048,256]{1,0:T(8,128)(2,1)} %cb_hbm.1, s32[1,1024]{1,0:T(1,128)} %bitcast.1), custom_call_target="tpu_custom_call" | custom-call | tf_op jit(solution)/shard_map/quantizer_backward/pallas_call | solution.py:401
  49.0 1.2 %write_out.1 = (f32[1024,256]{1,0:T(8,128)}, f32[512,256]{1,0:T(8,128)}) custom-call(f32[1024,256]{1,0:T(8,128)S(1)} %get-tuple-element.4.grad_tok_ref, f32[512,256]{1,0:T(8,128)S(1)} %get-tuple-element.5.grad_cb_ref), custom_call_target="tpu_custom_call" | custom-call | tf_op jit(solution)/shard_map/write_out/pallas_call | solution.py:442

commit v4 on v3

--- a/solution.py
+++ b/solution.py
@@ -90,6 +90,9 @@
             return (y * 16 + ((z + k) % RING) * 2 + core, x)
         return (((y + k) % RING) * 16 + z * 2 + core, x)
 
+    first = (("z", z), ("y", y))
+    second = (("y", y), ("z", z))
+
     loads = [
         pltpu.make_async_copy(src, dst, load_sem.at[i])
         for i, (src, dst) in enumerate(
@@ -98,9 +101,6 @@
     ]
     for load in loads:
         load.start()
-
-    first = (("z", z), ("y", y))
-    second = (("y", y), ("z", z))
 
     barrier = pltpu.get_barrier_semaphore()
 
@@ -301,10 +301,6 @@
     cb_send[1, low] = part[:mid].astype(BF16)
     near_copies[1].start()
     cb_own[1] = part[mid:]
-    for side, part in ((0, low), (1, high)):
-        far_copies[side].wait_recv()
-        cb_send[side, part] = (cb_own[side] + far_recv[side].astype(F32)).astype(BF16)
-        sum_copies[side].start()
     grad_cb_ref[...] = code_rows(0)
 
     ring_wait(sum_2, 3, second)
@@ -344,6 +340,10 @@
             final_copy(half, k).start()
     for half in range(2):
         final_forward(half, first[half][1], core).start()
+    for side, part in ((0, low), (1, high)):
+        far_copies[side].wait_recv()
+        cb_send[side, part] = (cb_own[side] + far_recv[side].astype(F32)).astype(BF16)
+        sum_copies[side].start()
     for k in reversed(FAR_FIRST):
         for half in range(2):
             final_arrival(half, k).wait_recv()

time: 50.3 us -> 47.6 us (0.946)
  Pallas kernels: 49.5 us -> 46.9 us
    pallas_call x1, Pallas kernels: 48.4 us -> 45.7 us  [shards(): pl.pallas_call(kernel, out_shape=shapes, in_specs=[hbm] * 4, out_specs=(v...]
where the time goes in v4:
time: 47.6 us; the launch traced here: 47.5 us
  Pallas kernels  46.9 us (99%)
  between operations  0.64 us (1%)
    pallas_call x1, Pallas kernels, shards(): pl.pallas_call(kernel, out_shape=shapes, in_specs=[hbm] * 4, out_specs=(v...  45.7 us
    pallas_call x1, Pallas kernels, shards(): pl.pallas_call(write, out_shape=shapes, in_specs=[vmem, vmem], out_specs=...  1.16 us

profile of v4, /device:TPU:1, one launch (start us, length us, event | category | flops | bytes accessed | tf_op | source)
XLA Modules:
  0.0 47.5 jit_solution(3321760976721776259)
XLA Ops:
  0.6 45.7 %quantizer_backward.1 = (f32[1024,256]{1,0:T(8,128)S(1)}, f32[512,256]{1,0:T(8,128)S(1)}) custom-call(bf16[1024,256]{1,0:T(8,128)(2,1)} %tok_hbm.1, bf16[1024,256]{1,0:T(8,128)(2,1)} %cot_hbm.1, bf16[2048,256]{1,0:T(8,128)(2,1)} %cb_hbm.1, s32[1,1024]{1,0:T(1,128)} %bitcast.1), custom_call_target="tpu_custom_call" | custom-call | tf_op jit(solution)/shard_map/quantizer_backward/pallas_call | solution.py:401
  46.3 1.2 %write_out.1 = (f32[1024,256]{1,0:T(8,128)}, f32[512,256]{1,0:T(8,128)}) custom-call(f32[1024,256]{1,0:T(8,128)S(1)} %get-tuple-element.4.grad_tok_ref, f32[512,256]{1,0:T(8,128)S(1)} %get-tuple-element.5.grad_cb_ref), custom_call_target="tpu_custom_call" | custom-call | tf_op jit(solution)/shard_map/write_out/pallas_call | solution.py:442

commit v5 on v4

--- a/solution.py
+++ b/solution.py
@@ -76,6 +76,7 @@
     core_recv,
     ring_send,
     ring_recv,
+    final_recv,
     x_send,
     x_recv,
 ):
@@ -115,23 +116,11 @@
     pl.semaphore_signal(barrier, inc=1, device_id=other, device_id_type=MESH)
 
     def ring_copy(buf, stage, half, axis, me, k, src=None):
-        slot = (me + k) % RING
         return pltpu.make_async_remote_copy(
-            src_ref=buf.at[half, me] if src is None else src.at[half, slot],
+            src_ref=buf.at[half, me] if src is None else src.at[half, (me + k) % RING],
             dst_ref=buf.at[half, me],
-            send_sem=ring_send.at[stage, half, slot],
-            recv_sem=ring_recv.at[stage, half, me],
-            device_id=along(axis, k),
-            device_id_type=MESH,
-        )
-
-    def ring_arrival(buf, stage, half, axis, me, k):
-        slot = (me + k) % RING
-        return pltpu.make_async_remote_copy(
-            src_ref=buf.at[half, slot],
-            dst_ref=buf.at[half, slot],
-            send_sem=ring_send.at[stage, half, slot],
-            recv_sem=ring_recv.at[stage, half, slot],
+            send_sem=ring_send.at[stage],
+            recv_sem=ring_recv.at[stage],
             device_id=along(axis, k),
             device_id_type=MESH,
         )
@@ -141,18 +130,16 @@
             for half in halves:
                 ring_copy(buf, stage, half, *order[half], k, src).start()
 
-    def ring_wait(buf, stage, order):
-        for k in reversed(FAR_FIRST):
-            for half in range(2):
-                ring_arrival(buf, stage, half, *order[half], k).wait_recv()
-
-    def ring_drain(buf, stage, order, src=None):
-        def step(k, carry):
-            for half in range(2):
-                ring_copy(buf, stage, half, *order[half], k, src).wait_send()
-            return carry
-
-        lax.fori_loop(1, RING, step, 0)
+    def ring_bytes(buf, stage):
+        blocks = buf.at[:, pl.ds(0, RING - 1)]
+        return pltpu.make_async_remote_copy(
+            src_ref=blocks,
+            dst_ref=blocks,
+            send_sem=ring_send.at[stage],
+            recv_sem=ring_recv.at[stage],
+            device_id=other,
+            device_id_type=MESH,
+        )
 
     def core_copy(src, dst, index):
         return pltpu.make_async_remote_copy(
@@ -227,7 +214,7 @@
 
     uv_ring(0)
 
-    ring_wait(stat_1, 0, first)
+    ring_bytes(stat_1, 0).wait_recv()
     for half in range(2):
         ring_top, ring_total, ring_weighted = combine([stat_1[half, j] for j in range(RING)])
         me = second[half][1]
@@ -242,7 +229,7 @@
     hot = jnp.where(hot, 1.0, 0.0).astype(BF16)
     direct[...] = jnp.dot(hot, cot_ref[...], preferred_element_type=F32)
 
-    ring_wait(stat_2, 2, second)
+    ring_bytes(stat_2, 2).wait_recv()
     state = [combine([stat_2[half, j] for j in range(RING)]) for half in range(2)]
     ratio = [w / t for _, t, w in state]
     local_scale = jnp.concatenate(
@@ -252,22 +239,22 @@
 
     low, high = pl.ds(0, QUARTER // 2), pl.ds(QUARTER // 2, QUARTER // 2)
 
-    def x_copy(src, dst, index, side):
+    def x_copy(src, dst, send, recv, side):
         return pltpu.make_async_remote_copy(
             src_ref=src,
             dst_ref=dst,
-            send_sem=x_send.at[index],
-            recv_sem=x_recv.at[index],
+            send_sem=x_send.at[send],
+            recv_sem=x_recv.at[recv],
             device_id=(code, (x + (1, x_size - 1)[side]) % x_size),
             device_id_type=MESH,
         )
 
-    far_copies = [x_copy(cb_send.at[2, part], far_recv.at[side], side, side) for side, part in ((0, low), (1, high))]
+    far_copies = [x_copy(cb_send.at[2, part], far_recv.at[side], 0, side, side) for side, part in ((0, low), (1, high))]
     near_copies = [
-        x_copy(cb_send.at[side, part], cb_recv.at[side, part], 2 + side, side) for side, part in ((0, high), (1, low))
+        x_copy(cb_send.at[side, part], cb_recv.at[side, part], 1, 2, side) for side, part in ((0, high), (1, low))
     ]
     sum_copies = [
-        x_copy(cb_send.at[side, part], cb_recv.at[side, part], 4 + side, side) for side, part in ((0, low), (1, high))
+        x_copy(cb_send.at[side, part], cb_recv.at[side, part], 1, 2, side) for side, part in ((0, low), (1, high))
     ]
 
     def code_rows(k):
@@ -279,7 +266,7 @@
     for copy in far_copies:
         copy.start()
 
-    ring_wait(uv_recv, 1, first)
+    ring_bytes(uv_recv, 1).wait_recv()
     for half in range(2):
         acc = jnp.zeros((ROWS, HALF), F32)
         for j in range(RING):
@@ -303,81 +290,57 @@
     cb_own[1] = part[mid:]
     grad_cb_ref[...] = code_rows(0)
 
-    ring_wait(sum_2, 3, second)
+    ring_bytes(sum_2, 3).wait_recv()
     for half in range(2):
         acc = functools.reduce(jnp.add, [sum_2[half, j].astype(F32) for j in range(RING)])
         final[core, half, first[half][1]] = acc.astype(BF16)
 
-    def final_copy(half, k):
+    def final_copy(half, k, slot):
         axis, me = first[half]
-        slot = (me + k) % RING
-        return pltpu.make_async_remote_copy(
-            src_ref=final.at[core, half, me],
-            dst_ref=final.at[core, half, me],
-            send_sem=ring_send.at[4, half, slot],
-            recv_sem=ring_recv.at[4, half, me],
-            device_id=along(axis, k),
-            device_id_type=MESH,
-        )
-
-    def final_arrival(half, k):
-        axis, me = first[half]
-        slot = (me + k) % RING
         return pltpu.make_async_remote_copy(
             src_ref=final.at[core, half, slot],
             dst_ref=final.at[core, half, slot],
-            send_sem=ring_send.at[4, half, slot],
-            recv_sem=ring_recv.at[4, half, slot],
+            send_sem=ring_send.at[4],
+            recv_sem=final_recv.at[half, slot],
             device_id=along(axis, k),
             device_id_type=MESH,
         )
 
-    def final_forward(half, slot, whose):
-        return core_copy(final.at[whose, half, slot], final.at[whose, half, slot], 3 + half * RING + slot)
+    def final_forward(half, slot):
+        return core_copy(final.at[core, half, slot], final.at[core, half, slot], 3)
 
     for k in FAR_FIRST:
         for half in range(2):
-            final_copy(half, k).start()
-    for half in range(2):
-        final_forward(half, first[half][1], core).start()
+            final_copy(half, k, first[half][1]).start()
+    for half in range(2):
+        final_forward(half, first[half][1]).start()
     for side, part in ((0, low), (1, high)):
         far_copies[side].wait_recv()
         cb_send[side, part] = (cb_own[side] + far_recv[side].astype(F32)).astype(BF16)
         sum_copies[side].start()
     for k in reversed(FAR_FIRST):
         for half in range(2):
-            final_arrival(half, k).wait_recv()
-            final_forward(half, (first[half][1] + k) % RING, core).start()
-
-    for copy in near_copies + sum_copies:
-        copy.wait_recv()
+            slot = (first[half][1] + k) % RING
+            final_copy(half, k, slot).wait_recv()
+            final_forward(half, slot).start()
+
+    x_copy(cb_send.at[pl.ds(0, 2)], cb_recv, 1, 2, 0).wait_recv()
     grad_cb_ref[...] += cb_recv[0].astype(F32) + cb_recv[1].astype(F32)
 
-    def final_end(k, carry):
-        for half in range(2):
-            final_forward(half, k, 1 - core).wait_recv()
-            final_forward(half, k, core).wait_send()
-        return carry
-
-    lax.fori_loop(0, RING, final_end, 0)
+    core_copy(final.at[core], final.at[1 - core], 3).wait()
     for half in range(2):
         for c in range(2):
             block = jnp.concatenate([final[c, half, j].astype(F32) for j in range(RING)], axis=0)
             grad_tok_ref[half * HALF : (half + 1) * HALF, c * 128 : (c + 1) * 128] = block.T
 
-    ring_drain(stat_1, 0, first)
-    ring_drain(uv_recv, 1, first, uv_send)
-    ring_drain(stat_2, 2, second)
-    ring_drain(sum_2, 3, second)
-
-    def final_drain(k, carry):
-        for half in range(2):
-            final_copy(half, k).wait_send()
-        return carry
-
-    lax.fori_loop(1, RING, final_drain, 0)
-    for copy in far_copies + near_copies + sum_copies:
-        copy.wait_send()
+    ring_bytes(stat_1, 0).wait_send()
+    ring_bytes(uv_send, 1).wait_send()
+    ring_bytes(stat_2, 2).wait_send()
+    ring_bytes(sum_2, 3).wait_send()
+
+    ring_bytes(final.at[core], 4).wait_send()
+    x_copy(cb_send.at[2], cb_send.at[2], 0, 0, 0).wait_send()
+    x_copy(cb_send.at[pl.ds(0, 2)], cb_recv, 1, 2, 0).wait_send()
 
 
 def write(grad_tok_ref, grad_cb_ref, tok_out, cb_out, sems):
@@ -427,12 +390,13 @@
             pltpu.VMEM((2, QUARTER, D), BF16),
             pltpu.VMEM((2, QUARTER // 2, D), BF16),
             pltpu.VMEM((2, QUARTER // 2, D), F32),
-            pltpu.SemaphoreType.DMA((3 + 2 * RING,)),
-            pltpu.SemaphoreType.DMA((3 + 2 * RING,)),
-            pltpu.SemaphoreType.DMA((5, 2, RING)),
-            pltpu.SemaphoreType.DMA((5, 2, RING)),
-            pltpu.SemaphoreType.DMA((6,)),
-            pltpu.SemaphoreType.DMA((6,)),
+            pltpu.SemaphoreType.DMA((4,)),
+            pltpu.SemaphoreType.DMA((4,)),
+            pltpu.SemaphoreType.DMA((5,)),
+            pltpu.SemaphoreType.DMA((4,)),
+            pltpu.SemaphoreType.DMA((2, RING)),
+            pltpu.SemaphoreType.DMA((2,)),
+            pltpu.SemaphoreType.DMA((3,)),
         ],
         compiler_params=pltpu.CompilerParams(
             collective_id=0, has_side_effects=True, vmem_limit_bytes=VMEM_LIMIT

time: 47.6 us -> 45.3 us (0.952)
  Pallas kernels: 46.9 us -> 44.5 us
    pallas_call x1, Pallas kernels: 45.7 us -> 43.3 us  [shards(): pl.pallas_call(kernel, out_shape=shapes, in_specs=[hbm] * 4, out_specs=(v...]
where the time goes in v5:
time: 45.3 us; the launch traced here: 45.1 us
  Pallas kernels  44.5 us (98%)
  between operations  0.64 us (1%)
    pallas_call x1, Pallas kernels, shards(): pl.pallas_call(kernel, out_shape=shapes, in_specs=[hbm] * 4, out_specs=(v...  43.3 us
    pallas_call x1, Pallas kernels, shards(): pl.pallas_call(write, out_shape=shapes, in_specs=[vmem, vmem], out_specs=...  1.16 us

profile of v5, /device:TPU:1, one launch (start us, length us, event | category | flops | bytes accessed | tf_op | source)
XLA Modules:
  0.0 45.1 jit_solution(3334085542276773361)
XLA Ops:
  0.6 43.3 %quantizer_backward.1 = (f32[1024,256]{1,0:T(8,128)S(1)}, f32[512,256]{1,0:T(8,128)S(1)}) custom-call(bf16[1024,256]{1,0:T(8,128)(2,1)} %tok_hbm.1, bf16[1024,256]{1,0:T(8,128)(2,1)} %cot_hbm.1, bf16[2048,256]{1,0:T(8,128)(2,1)} %cb_hbm.1, s32[1,1024]{1,0:T(1,128)} %bitcast.1), custom_call_target="tpu_custom_call" | custom-call | tf_op jit(solution)/shard_map/quantizer_backward/pallas_call | solution.py:364
  44.0 1.2 %write_out.1 = (f32[1024,256]{1,0:T(8,128)}, f32[512,256]{1,0:T(8,128)}) custom-call(f32[1024,256]{1,0:T(8,128)S(1)} %get-tuple-element.4.grad_tok_ref, f32[512,256]{1,0:T(8,128)S(1)} %get-tuple-element.5.grad_cb_ref), custom_call_target="tpu_custom_call" | custom-call | tf_op jit(solution)/shard_map/write_out/pallas_call | solution.py:406

commit v6 on v5

--- a/solution.py
+++ b/solution.py
@@ -11,10 +11,12 @@
 F32 = jnp.float32
 BF16 = jnp.bfloat16
 NT = (((1,), (1,)), ((), ()))
+TN = (((0,), (0,)), ((), ()))
 
 RING = 8
 FAR_FIRST = (4, 3, 5, 2, 6, 1, 7)
 TOK = 1024
+SPAN = TOK // 4
 HALF = TOK // 2
 CODES = 2048
 D = 256
@@ -57,7 +59,7 @@
     expo,
     back,
     direct,
-    cbt,
+    uv_first,
     uv_own,
     uv_other,
     uv_send,
@@ -130,8 +132,8 @@
             for half in halves:
                 ring_copy(buf, stage, half, *order[half], k, src).start()
 
-    def ring_bytes(buf, stage):
-        blocks = buf.at[:, pl.ds(0, RING - 1)]
+    def ring_bytes(buf, stage, half=None):
+        blocks = buf.at[slice(None) if half is None else half, pl.ds(0, RING - 1)]
         return pltpu.make_async_remote_copy(
             src_ref=blocks,
             dst_ref=blocks,
@@ -165,6 +167,7 @@
     expo[...] = e
     total = jnp.sum(fold(e, jnp.sum), axis=0, keepdims=True)
     weighted = jnp.sum(fold(e * back[...], jnp.sum), axis=0, keepdims=True)
+    own_mean = weighted / total
 
     for half in range(2):
         span = slice(half * HALF, (half + 1) * HALF)
@@ -175,7 +178,15 @@
     stat_copy = core_copy(stat_own, stat_other, 0)
     stat_copy.start()
 
-    cbt[...] = cb_ref[...].T
+    def uv_terms(quarter):
+        span = slice(quarter * SPAN, (quarter + 1) * SPAN)
+        e = expo[:, span]
+        u = (e * (back[:, span] - own_mean[:, span])).astype(BF16)
+        return [
+            lax.dot_general(cb_ref[...], weight, TN, preferred_element_type=F32) for weight in (u, e.astype(BF16))
+        ]
+
+    uv_first[0], uv_first[1] = uv_terms(0)
     stat_copy.wait()
 
     scale, mean = [], []
@@ -190,29 +201,40 @@
         mean.append(to_row(pair_weighted / pair_total))
     ring_start(stat_1, 0, first)
 
-    uv_copies = [core_copy(uv_own.at[half, 1 - core], uv_other.at[half], 1 + half) for half in range(2)]
-
-    for half in range(2):
-        span = slice(half * HALF, (half + 1) * HALF)
-        e = expo[:, span] * scale[half]
-        u = (e * (back[:, span] - mean[half])).astype(BF16)
-        for which, weight in ((0, u), (1, e.astype(BF16))):
-            value = jnp.dot(cbt[...], weight, preferred_element_type=F32).astype(BF16)
+    scale = jnp.concatenate(scale, axis=1)
+    shift = own_mean - jnp.concatenate(mean, axis=1)
+    uv_copies = [core_copy(uv_own.at[q, 1 - core], uv_other.at[q], 1 + q) for q in range(4)]
+
+    def uv_chip(quarter, u, v):
+        span = slice(quarter * SPAN, (quarter + 1) * SPAN)
+        u = (u + shift[:, span] * v) * scale[:, span]
+        v = v * scale[:, span]
+        for which, value in ((0, u), (1, v)):
             for c in range(2):
-                uv_own[half, c, which] = value[c * 128 : (c + 1) * 128]
-        uv_copies[half].start()
+                uv_own[quarter, c, which] = value[c * 128 : (c + 1) * 128].astype(BF16)
+        uv_copies[quarter].start()
+
+    def uv_sum(quarter):
+        uv_copies[quarter].wait()
+        half, span = quarter // 2, slice(quarter % 2 * SPAN, (quarter % 2 + 1) * SPAN)
+        for which in range(2):
+            both = uv_own[quarter, core, which].astype(F32) + uv_other[quarter, which].astype(F32)
+            for k in range(RING):
+                uv_send[half, k, which, :, span] = both[k * ROWS : (k + 1) * ROWS].astype(BF16)
 
     def uv_ring(half):
-        uv_copies[half].wait()
         me = first[half][1]
-        for which in range(2):
-            both = uv_own[half, core, which].astype(F32) + uv_other[half, which].astype(F32)
-            for k in range(RING):
-                uv_send[half, k, which] = both[k * ROWS : (k + 1) * ROWS].astype(BF16)
         uv_recv[half, me] = uv_send[half, me]
-        ring_start(uv_recv, 1, first, uv_send, (half,))
-
+        ring_start(uv_recv, 1 + half, first, uv_send, (half,))
+
+    uv_chip(0, uv_first[0], uv_first[1])
+    uv_chip(1, *uv_terms(1))
+    uv_chip(2, *uv_terms(2))
+    uv_sum(0)
+    uv_sum(1)
     uv_ring(0)
+    uv_chip(3, *uv_terms(3))
+    uv_sum(2)
 
     ring_bytes(stat_1, 0).wait_recv()
     for half in range(2):
@@ -221,7 +243,8 @@
         stat_2[half, me, 0:4] = ring_top
         stat_2[half, me, 4:8] = ring_total
         stat_2[half, me, 8:12] = ring_weighted
-    ring_start(stat_2, 2, second)
+    ring_start(stat_2, 3, second)
+    uv_sum(3)
     uv_ring(1)
 
     loads[3].wait()
@@ -229,7 +252,7 @@
     hot = jnp.where(hot, 1.0, 0.0).astype(BF16)
     direct[...] = jnp.dot(hot, cot_ref[...], preferred_element_type=F32)
 
-    ring_bytes(stat_2, 2).wait_recv()
+    ring_bytes(stat_2, 3).wait_recv()
     state = [combine([stat_2[half, j] for j in range(RING)]) for half in range(2)]
     ratio = [w / t for _, t, w in state]
     local_scale = jnp.concatenate(
@@ -266,18 +289,18 @@
     for copy in far_copies:
         copy.start()
 
-    ring_bytes(uv_recv, 1).wait_recv()
-    for half in range(2):
+    for half in range(2):
+        ring_bytes(uv_recv, 1 + half, half).wait_recv()
         acc = jnp.zeros((ROWS, HALF), F32)
         for j in range(RING):
             peer = stat_1[half, j]
             factor = jnp.exp(peer[0:4] - state[half][0]) / state[half][1]
-            shift = peer[8:12] / peer[4:8] - ratio[half]
+            peer_shift = peer[8:12] / peer[4:8] - ratio[half]
             acc = acc + to_row(factor) * (
-                uv_recv[half, j, 0].astype(F32) + to_row(shift) * uv_recv[half, j, 1].astype(F32)
+                uv_recv[half, j, 0].astype(F32) + to_row(peer_shift) * uv_recv[half, j, 1].astype(F32)
             )
         sum_2[half, second[half][1]] = acc.astype(BF16)
-    ring_start(sum_2, 3, second)
+        ring_start(sum_2, 4 + half, second, None, (half,))
 
     mid = QUARTER // 2
     part = code_rows(1)
@@ -290,30 +313,28 @@
     cb_own[1] = part[mid:]
     grad_cb_ref[...] = code_rows(0)
 
-    ring_bytes(sum_2, 3).wait_recv()
-    for half in range(2):
-        acc = functools.reduce(jnp.add, [sum_2[half, j].astype(F32) for j in range(RING)])
-        final[core, half, first[half][1]] = acc.astype(BF16)
-
     def final_copy(half, k, slot):
         axis, me = first[half]
         return pltpu.make_async_remote_copy(
             src_ref=final.at[core, half, slot],
             dst_ref=final.at[core, half, slot],
-            send_sem=ring_send.at[4],
+            send_sem=ring_send.at[6 + half],
             recv_sem=final_recv.at[half, slot],
             device_id=along(axis, k),
             device_id_type=MESH,
         )
 
     def final_forward(half, slot):
-        return core_copy(final.at[core, half, slot], final.at[core, half, slot], 3)
-
-    for k in FAR_FIRST:
-        for half in range(2):
-            final_copy(half, k, first[half][1]).start()
-    for half in range(2):
-        final_forward(half, first[half][1]).start()
+        return core_copy(final.at[core, half, slot], final.at[core, half, slot], 5)
+
+    for half in range(2):
+        ring_bytes(sum_2, 4 + half, half).wait_recv()
+        me = first[half][1]
+        acc = functools.reduce(jnp.add, [sum_2[half, j].astype(F32) for j in range(RING)])
+        final[core, half, me] = acc.astype(BF16)
+        for k in FAR_FIRST:
+            final_copy(half, k, me).start()
+        final_forward(half, me).start()
     for side, part in ((0, low), (1, high)):
         far_copies[side].wait_recv()
         cb_send[side, part] = (cb_own[side] + far_recv[side].astype(F32)).astype(BF16)
@@ -327,18 +348,18 @@
     x_copy(cb_send.at[pl.ds(0, 2)], cb_recv, 1, 2, 0).wait_recv()
     grad_cb_ref[...] += cb_recv[0].astype(F32) + cb_recv[1].astype(F32)
 
-    core_copy(final.at[core], final.at[1 - core], 3).wait()
+    core_copy(final.at[core], final.at[1 - core], 5).wait()
     for half in range(2):
         for c in range(2):
             block = jnp.concatenate([final[c, half, j].astype(F32) for j in range(RING)], axis=0)
             grad_tok_ref[half * HALF : (half + 1) * HALF, c * 128 : (c + 1) * 128] = block.T
 
     ring_bytes(stat_1, 0).wait_send()
-    ring_bytes(uv_send, 1).wait_send()
-    ring_bytes(stat_2, 2).wait_send()
-    ring_bytes(sum_2, 3).wait_send()
-
-    ring_bytes(final.at[core], 4).wait_send()
+    ring_bytes(stat_2, 3).wait_send()
+    for half in range(2):
+        ring_bytes(uv_send, 1 + half, half).wait_send()
+        ring_bytes(sum_2, 4 + half, half).wait_send()
+        ring_bytes(final.at[core], 6 + half, half).wait_send()
     x_copy(cb_send.at[2], cb_send.at[2], 0, 0, 0).wait_send()
     x_copy(cb_send.at[pl.ds(0, 2)], cb_recv, 1, 2, 0).wait_send()
 
@@ -375,9 +396,9 @@
             pltpu.VMEM((CODES, TOK), F32),
             pltpu.VMEM((CODES, TOK), F32),
             pltpu.VMEM((CODES, D), F32),
-            pltpu.VMEM((D, CODES), BF16),
-            pltpu.VMEM((2, 2, 2, 128, HALF), BF16),
-            pltpu.VMEM((2, 2, 128, HALF), BF16),
+            pltpu.VMEM((2, D, SPAN), F32),
+            pltpu.VMEM((4, 2, 2, 128, SPAN), BF16),
+            pltpu.VMEM((4, 2, 128, SPAN), BF16),
             pltpu.VMEM((2, RING, 2, ROWS, HALF), BF16),
             pltpu.VMEM((2, RING, 2, ROWS, HALF), BF16),
             pltpu.VMEM((2, 12, 128), F32),
@@ -390,10 +411,10 @@
             pltpu.VMEM((2, QUARTER, D), BF16),
             pltpu.VMEM((2, QUARTER // 2, D), BF16),
             pltpu.VMEM((2, QUARTER // 2, D), F32),
-            pltpu.SemaphoreType.DMA((4,)),
-            pltpu.SemaphoreType.DMA((4,)),
-            pltpu.SemaphoreType.DMA((5,)),
-            pltpu.SemaphoreType.DMA((4,)),
+            pltpu.SemaphoreType.DMA((6,)),
+            pltpu.SemaphoreType.DMA((6,)),
+            pltpu.SemaphoreType.DMA((8,)),
+            pltpu.SemaphoreType.DMA((6,)),
             pltpu.SemaphoreType.DMA((2, RING)),
             pltpu.SemaphoreType.DMA((2,)),
             pltpu.SemaphoreType.DMA((3,)),

time: 45.3 us -> 46.3 us (1.022)
  Pallas kernels: 44.5 us -> 45.5 us
    pallas_call x1, Pallas kernels: 43.3 us -> 44.3 us  [shards(): pl.pallas_call(kernel, out_shape=shapes, in_specs=[hbm] * 4, out_specs=(v...]
where the time goes in v6:
time: 46.3 us; the launch traced here: 46.1 us
  Pallas kernels  45.5 us (98%)
  between operations  0.64 us (1%)
    pallas_call x1, Pallas kernels, shards(): pl.pallas_call(kernel, out_shape=shapes, in_specs=[hbm] * 4, out_specs=(v...  44.3 us
    pallas_call x1, Pallas kernels, shards(): pl.pallas_call(write, out_shape=shapes, in_specs=[vmem, vmem], out_specs=...  1.16 us

profile of v6, /device:TPU:1, one launch (start us, length us, event | category | flops | bytes accessed | tf_op | source)
XLA Modules:
  0.0 46.1 jit_solution(11478972114370125967)
XLA Ops:
  0.6 44.3 %quantizer_backward.1 = (f32[1024,256]{1,0:T(8,128)S(1)}, f32[512,256]{1,0:T(8,128)S(1)}) custom-call(bf16[1024,256]{1,0:T(8,128)(2,1)} %tok_hbm.1, bf16[1024,256]{1,0:T(8,128)(2,1)} %cot_hbm.1, bf16[2048,256]{1,0:T(8,128)(2,1)} %cb_hbm.1, s32[1,1024]{1,0:T(1,128)} %bitcast.1), custom_call_target="tpu_custom_call" | custom-call | tf_op jit(solution)/shard_map/quantizer_backward/pallas_call | solution.py:385
  44.9 1.2 %write_out.1 = (f32[1024,256]{1,0:T(8,128)}, f32[512,256]{1,0:T(8,128)}) custom-call(f32[1024,256]{1,0:T(8,128)S(1)} %get-tuple-element.4.grad_tok_ref, f32[512,256]{1,0:T(8,128)S(1)} %get-tuple-element.5.grad_cb_ref), custom_call_target="tpu_custom_call" | custom-call | tf_op jit(solution)/shard_map/write_out/pallas_call | solution.py:427

commit v7 on v5

--- a/solution.py
+++ b/solution.py
@@ -58,6 +58,7 @@
     back,
     direct,
     cbt,
+    v_first,
     uv_own,
     uv_other,
     uv_send,
@@ -175,7 +176,15 @@
     stat_copy = core_copy(stat_own, stat_other, 0)
     stat_copy.start()
 
-    cbt[...] = cb_ref[...].T
+    eye = lax.broadcasted_iota(jnp.int32, (D, D), 0) == lax.broadcasted_iota(jnp.int32, (D, D), 1)
+    eye = jnp.where(eye, 1.0, 0.0).astype(BF16)
+    cbt[...] = lax.dot_general(eye, cb_ref[...], NT, preferred_element_type=F32).astype(BF16)
+
+    def v_terms(half):
+        weight = expo[:, half * HALF : (half + 1) * HALF].astype(BF16)
+        return jnp.dot(cbt[...], weight, preferred_element_type=F32)
+
+    v_first[...] = v_terms(0)
     stat_copy.wait()
 
     scale, mean = [], []
@@ -190,29 +199,36 @@
         mean.append(to_row(pair_weighted / pair_total))
     ring_start(stat_1, 0, first)
 
-    uv_copies = [core_copy(uv_own.at[half, 1 - core], uv_other.at[half], 1 + half) for half in range(2)]
-
-    for half in range(2):
+    uv_copies = [
+        [core_copy(uv_own.at[which, half, 1 - core], uv_other.at[which, half], 1 + 2 * which + half) for half in range(2)]
+        for which in range(2)
+    ]
+
+    def uv_chip(which, half, value):
+        for c in range(2):
+            uv_own[which, half, c] = value[c * 128 : (c + 1) * 128].astype(BF16)
+        uv_copies[which][half].start()
+
+    def u_terms(half):
         span = slice(half * HALF, (half + 1) * HALF)
-        e = expo[:, span] * scale[half]
-        u = (e * (back[:, span] - mean[half])).astype(BF16)
-        for which, weight in ((0, u), (1, e.astype(BF16))):
-            value = jnp.dot(cbt[...], weight, preferred_element_type=F32).astype(BF16)
-            for c in range(2):
-                uv_own[half, c, which] = value[c * 128 : (c + 1) * 128]
-        uv_copies[half].start()
-
-    def uv_ring(half):
-        uv_copies[half].wait()
-        me = first[half][1]
-        for which in range(2):
-            both = uv_own[half, core, which].astype(F32) + uv_other[half, which].astype(F32)
-            for k in range(RING):
-                uv_send[half, k, which] = both[k * ROWS : (k + 1) * ROWS].astype(BF16)
-        uv_recv[half, me] = uv_send[half, me]
-        ring_start(uv_recv, 1, first, uv_send, (half,))
-
-    uv_ring(0)
+        weight = (expo[:, span] * scale[half] * (back[:, span] - mean[half])).astype(BF16)
+        return jnp.dot(cbt[...], weight, preferred_element_type=F32)
+
+    def uv_sum(which, half):
+        uv_copies[which][half].wait()
+        both = uv_own[which, half, core].astype(F32) + uv_other[which, half].astype(F32)
+        for k in range(RING):
+            uv_send[which, half, k] = both[k * ROWS : (k + 1) * ROWS].astype(BF16)
+        uv_recv[which, half, first[half][1]] = uv_send[which, half, first[half][1]]
+
+    uv_chip(1, 0, v_first[...] * scale[0])
+    uv_chip(1, 1, v_terms(1) * scale[1])
+    uv_chip(0, 0, u_terms(0))
+    uv_sum(1, 0)
+    uv_sum(1, 1)
+    ring_start(uv_recv.at[1], 1, first, uv_send.at[1])
+    uv_chip(0, 1, u_terms(1))
+    uv_sum(0, 0)
 
     ring_bytes(stat_1, 0).wait_recv()
     for half in range(2):
@@ -222,7 +238,8 @@
         stat_2[half, me, 4:8] = ring_total
         stat_2[half, me, 8:12] = ring_weighted
     ring_start(stat_2, 2, second)
-    uv_ring(1)
+    uv_sum(0, 1)
+    ring_start(uv_recv.at[0], 5, first, uv_send.at[0])
 
     loads[3].wait()
     hot = lax.broadcasted_iota(jnp.int32, (CODES, TOK), 0) == idx_ref[...] - code * CODES
@@ -266,7 +283,8 @@
     for copy in far_copies:
         copy.start()
 
-    ring_bytes(uv_recv, 1).wait_recv()
+    ring_bytes(uv_recv.at[1], 1).wait_recv()
+    ring_bytes(uv_recv.at[0], 5).wait_recv()
     for half in range(2):
         acc = jnp.zeros((ROWS, HALF), F32)
         for j in range(RING):
@@ -274,7 +292,7 @@
             factor = jnp.exp(peer[0:4] - state[half][0]) / state[half][1]
             shift = peer[8:12] / peer[4:8] - ratio[half]
             acc = acc + to_row(factor) * (
-                uv_recv[half, j, 0].astype(F32) + to_row(shift) * uv_recv[half, j, 1].astype(F32)
+                uv_recv[0, half, j].astype(F32) + to_row(shift) * uv_recv[1, half, j].astype(F32)
             )
         sum_2[half, second[half][1]] = acc.astype(BF16)
     ring_start(sum_2, 3, second)
@@ -307,7 +325,7 @@
         )
 
     def final_forward(half, slot):
-        return core_copy(final.at[core, half, slot], final.at[core, half, slot], 3)
+        return core_copy(final.at[core, half, slot], final.at[core, half, slot], 5)
 
     for k in FAR_FIRST:
         for half in range(2):
@@ -327,14 +345,15 @@
     x_copy(cb_send.at[pl.ds(0, 2)], cb_recv, 1, 2, 0).wait_recv()
     grad_cb_ref[...] += cb_recv[0].astype(F32) + cb_recv[1].astype(F32)
 
-    core_copy(final.at[core], final.at[1 - core], 3).wait()
+    core_copy(final.at[core], final.at[1 - core], 5).wait()
     for half in range(2):
         for c in range(2):
             block = jnp.concatenate([final[c, half, j].astype(F32) for j in range(RING)], axis=0)
             grad_tok_ref[half * HALF : (half + 1) * HALF, c * 128 : (c + 1) * 128] = block.T
 
     ring_bytes(stat_1, 0).wait_send()
-    ring_bytes(uv_send, 1).wait_send()
+    ring_bytes(uv_send.at[1], 1).wait_send()
+    ring_bytes(uv_send.at[0], 5).wait_send()
     ring_bytes(stat_2, 2).wait_send()
     ring_bytes(sum_2, 3).wait_send()
 
@@ -376,10 +395,11 @@
             pltpu.VMEM((CODES, TOK), F32),
             pltpu.VMEM((CODES, D), F32),
             pltpu.VMEM((D, CODES), BF16),
+            pltpu.VMEM((D, HALF), F32),
             pltpu.VMEM((2, 2, 2, 128, HALF), BF16),
             pltpu.VMEM((2, 2, 128, HALF), BF16),
-            pltpu.VMEM((2, RING, 2, ROWS, HALF), BF16),
-            pltpu.VMEM((2, RING, 2, ROWS, HALF), BF16),
+            pltpu.VMEM((2, 2, RING, ROWS, HALF), BF16),
+            pltpu.VMEM((2, 2, RING, ROWS, HALF), BF16),
             pltpu.VMEM((2, 12, 128), F32),
             pltpu.VMEM((2, 12, 128), F32),
             pltpu.VMEM((2, RING, 12, 128), F32),
@@ -390,10 +410,10 @@
             pltpu.VMEM((2, QUARTER, D), BF16),
             pltpu.VMEM((2, QUARTER // 2, D), BF16),
             pltpu.VMEM((2, QUARTER // 2, D), F32),
-            pltpu.SemaphoreType.DMA((4,)),
-            pltpu.SemaphoreType.DMA((4,)),
-            pltpu.SemaphoreType.DMA((5,)),
-            pltpu.SemaphoreType.DMA((4,)),
+            pltpu.SemaphoreType.DMA((6,)),
+            pltpu.SemaphoreType.DMA((6,)),
+            pltpu.SemaphoreType.DMA((6,)),
+            pltpu.SemaphoreType.DMA((6,)),
             pltpu.SemaphoreType.DMA((2, RING)),
             pltpu.SemaphoreType.DMA((2,)),
             pltpu.SemaphoreType.DMA((3,)),

time: 45.3 us -> 43.7 us (0.965)
  Pallas kernels: 44.5 us -> 42.9 us
    pallas_call x1, Pallas kernels: 43.3 us -> 41.8 us  [shards(): pl.pallas_call(kernel, out_shape=shapes, in_specs=[hbm] * 4, out_specs=(v...]
where the time goes in v7:
time: 43.7 us; the launch traced here: 43.6 us
  Pallas kernels  42.9 us (98%)
  between operations  0.64 us (1%)
    pallas_call x1, Pallas kernels, shards(): pl.pallas_call(kernel, out_shape=shapes, in_specs=[hbm] * 4, out_specs=(v...  41.8 us
    pallas_call x1, Pallas kernels, shards(): pl.pallas_call(write, out_shape=shapes, in_specs=[vmem, vmem], out_specs=...  1.16 us

profile of v7, /device:TPU:1, one launch (start us, length us, event | category | flops | bytes accessed | tf_op | source)
XLA Modules:
  0.0 43.6 jit_solution(14463781617512276041)
XLA Ops:
  0.6 41.8 %quantizer_backward.1 = (f32[1024,256]{1,0:T(8,128)S(1)}, f32[512,256]{1,0:T(8,128)S(1)}) custom-call(bf16[1024,256]{1,0:T(8,128)(2,1)} %tok_hbm.1, bf16[1024,256]{1,0:T(8,128)(2,1)} %cot_hbm.1, bf16[2048,256]{1,0:T(8,128)(2,1)} %cb_hbm.1, s32[1,1024]{1,0:T(1,128)} %bitcast.1), custom_call_target="tpu_custom_call" | custom-call | tf_op jit(solution)/shard_map/quantizer_backward/pallas_call | solution.py:383
  42.4 1.2 %write_out.1 = (f32[1024,256]{1,0:T(8,128)}, f32[512,256]{1,0:T(8,128)}) custom-call(f32[1024,256]{1,0:T(8,128)S(1)} %get-tuple-element.4.grad_tok_ref, f32[512,256]{1,0:T(8,128)S(1)} %get-tuple-element.5.grad_cb_ref), custom_call_target="tpu_custom_call" | custom-call | tf_op jit(solution)/shard_map/write_out/pallas_call | solution.py:426

commit v8 on v7

--- a/solution.py
+++ b/solution.py
@@ -224,10 +224,10 @@
     uv_chip(1, 0, v_first[...] * scale[0])
     uv_chip(1, 1, v_terms(1) * scale[1])
     uv_chip(0, 0, u_terms(0))
+    uv_chip(0, 1, u_terms(1))
     uv_sum(1, 0)
     uv_sum(1, 1)
     ring_start(uv_recv.at[1], 1, first, uv_send.at[1])
-    uv_chip(0, 1, u_terms(1))
     uv_sum(0, 0)
 
     ring_bytes(stat_1, 0).wait_recv()
@@ -238,8 +238,9 @@
         stat_2[half, me, 4:8] = ring_total
         stat_2[half, me, 8:12] = ring_weighted
     ring_start(stat_2, 2, second)
+    ring_start(uv_recv.at[0], 5, first, uv_send.at[0], (0,))
     uv_sum(0, 1)
-    ring_start(uv_recv.at[0], 5, first, uv_send.at[0])
+    ring_start(uv_recv.at[0], 5, first, uv_send.at[0], (1,))
 
     loads[3].wait()
     hot = lax.broadcasted_iota(jnp.int32, (CODES, TOK), 0) == idx_ref[...] - code * CODES
@@ -278,10 +279,6 @@
         rows = pl.ds(pl.multiple_of(((x + k) % x_size) * QUARTER, QUARTER), QUARTER)
         grad = (expo[rows] * local_scale * (back[rows] - ratio_row)).astype(BF16)
         return jnp.dot(grad, tok_ref[...], preferred_element_type=F32) + direct[rows]
-
-    cb_send[2] = code_rows(2).astype(BF16)
-    for copy in far_copies:
-        copy.start()
 
     ring_bytes(uv_recv.at[1], 1).wait_recv()
     ring_bytes(uv_recv.at[0], 5).wait_recv()
@@ -297,6 +294,11 @@
         sum_2[half, second[half][1]] = acc.astype(BF16)
     ring_start(sum_2, 3, second)
 
+    cb_send[2] = code_rows(2).astype(BF16)
+    for copy in far_copies:
+        copy.start()
+
+
     mid = QUARTER // 2
     part = code_rows(1)
     cb_send[0, high] = part[mid:].astype(BF16)
@@ -342,14 +344,17 @@
             final_copy(half, k, slot).wait_recv()
             final_forward(half, slot).start()
 
+    def turn_rows(c):
+        for half in range(2):
+            block = jnp.concatenate([final[c, half, j].astype(F32) for j in range(RING)], axis=0)
+            lanes = pl.ds(pl.multiple_of(c * 128, 128), 128)
+            grad_tok_ref[half * HALF : (half + 1) * HALF, lanes] = block.T
+
+    turn_rows(core)
     x_copy(cb_send.at[pl.ds(0, 2)], cb_recv, 1, 2, 0).wait_recv()
     grad_cb_ref[...] += cb_recv[0].astype(F32) + cb_recv[1].astype(F32)
-
     core_copy(final.at[core], final.at[1 - core], 5).wait()
-    for half in range(2):
-        for c in range(2):
-            block = jnp.concatenate([final[c, half, j].astype(F32) for j in range(RING)], axis=0)
-            grad_tok_ref[half * HALF : (half + 1) * HALF, c * 128 : (c + 1) * 128] = block.T
+    turn_rows(1 - core)
 
     ring_bytes(stat_1, 0).wait_send()
     ring_bytes(uv_send.at[1], 1).wait_send()

time: 43.7 us -> 44 us (level)
  no operation moved by 1% of the time
where the time goes in v8:
time: 44 us; the launch traced here: 43.8 us
  Pallas kernels  43.2 us (98%)
  between operations  0.64 us (1%)
    pallas_call x1, Pallas kernels, shards(): pl.pallas_call(kernel, out_shape=shapes, in_specs=[hbm] * 4, out_specs=(v...  42 us
    pallas_call x1, Pallas kernels, shards(): pl.pallas_call(write, out_shape=shapes, in_specs=[vmem, vmem], out_specs=...  1.16 us

profile of v8, /device:TPU:1, one launch (start us, length us, event | category | flops | bytes accessed | tf_op | source)
XLA Modules:
  0.0 43.8 jit_solution(13978913031201222829)
XLA Ops:
  0.6 42.0 %quantizer_backward.1 = (f32[1024,256]{1,0:T(8,128)S(1)}, f32[512,256]{1,0:T(8,128)S(1)}) custom-call(bf16[1024,256]{1,0:T(8,128)(2,1)} %tok_hbm.1, bf16[1024,256]{1,0:T(8,128)(2,1)} %cot_hbm.1, bf16[2048,256]{1,0:T(8,128)(2,1)} %cb_hbm.1, s32[1,1024]{1,0:T(1,128)} %bitcast.1), custom_call_target="tpu_custom_call" | custom-call | tf_op jit(solution)/shard_map/quantizer_backward/pallas_call | solution.py:388
  42.7 1.2 %write_out.1 = (f32[1024,256]{1,0:T(8,128)}, f32[512,256]{1,0:T(8,128)}) custom-call(f32[1024,256]{1,0:T(8,128)S(1)} %get-tuple-element.4.grad_tok_ref, f32[512,256]{1,0:T(8,128)S(1)} %get-tuple-element.5.grad_cb_ref), custom_call_target="tpu_custom_call" | custom-call | tf_op jit(solution)/shard_map/write_out/pallas_call | solution.py:431

commit v9 on v8

--- a/solution.py
+++ b/solution.py
@@ -67,6 +67,7 @@
     stat_other,
     stat_1,
     stat_2,
+    mix,
     sum_2,
     final,
     cb_send,
@@ -280,17 +281,20 @@
         grad = (expo[rows] * local_scale * (back[rows] - ratio_row)).astype(BF16)
         return jnp.dot(grad, tok_ref[...], preferred_element_type=F32) + direct[rows]
 
-    ring_bytes(uv_recv.at[1], 1).wait_recv()
-    ring_bytes(uv_recv.at[0], 5).wait_recv()
-    for half in range(2):
-        acc = jnp.zeros((ROWS, HALF), F32)
+    for half in range(2):
         for j in range(RING):
             peer = stat_1[half, j]
             factor = jnp.exp(peer[0:4] - state[half][0]) / state[half][1]
             shift = peer[8:12] / peer[4:8] - ratio[half]
-            acc = acc + to_row(factor) * (
-                uv_recv[0, half, j].astype(F32) + to_row(shift) * uv_recv[1, half, j].astype(F32)
-            )
+            mix[half, j, 0:1] = to_row(factor)
+            mix[half, j, 1:2] = to_row(factor * shift)
+    ring_bytes(uv_recv.at[1], 1).wait_recv()
+    ring_bytes(uv_recv.at[0], 5).wait_recv()
+    for half in range(2):
+        acc = jnp.zeros((ROWS, HALF), F32)
+        for j in range(RING):
+            acc = acc + mix[half, j, 0:1] * uv_recv[0, half, j].astype(F32)
+            acc = acc + mix[half, j, 1:2] * uv_recv[1, half, j].astype(F32)
         sum_2[half, second[half][1]] = acc.astype(BF16)
     ring_start(sum_2, 3, second)
 
@@ -321,7 +325,7 @@
             src_ref=final.at[core, half, slot],
             dst_ref=final.at[core, half, slot],
             send_sem=ring_send.at[4],
-            recv_sem=final_recv.at[half, slot],
+            recv_sem=final_recv.at[k],
             device_id=along(axis, k),
             device_id_type=MESH,
         )
@@ -339,10 +343,17 @@
         cb_send[side, part] = (cb_own[side] + far_recv[side].astype(F32)).astype(BF16)
         sum_copies[side].start()
     for k in reversed(FAR_FIRST):
+        both = final.at[core, :, 0]
+        pltpu.make_async_remote_copy(
+            src_ref=both,
+            dst_ref=both,
+            send_sem=ring_send.at[4],
+            recv_sem=final_recv.at[RING - k],
+            device_id=other,
+            device_id_type=MESH,
+        ).wait_recv()
         for half in range(2):
-            slot = (first[half][1] + k) % RING
-            final_copy(half, k, slot).wait_recv()
-            final_forward(half, slot).start()
+            final_forward(half, (first[half][1] + k) % RING).start()
 
     def turn_rows(c):
         for half in range(2):
@@ -409,6 +420,7 @@
             pltpu.VMEM((2, 12, 128), F32),
             pltpu.VMEM((2, RING, 12, 128), F32),
             pltpu.VMEM((2, RING, 12, 128), F32),
+            pltpu.VMEM((2, RING, 2, HALF), F32),
             pltpu.VMEM((2, RING, ROWS, HALF), BF16),
             pltpu.VMEM((2, 2, RING, ROWS, HALF), BF16),
             pltpu.VMEM((3, QUARTER, D), BF16),
@@ -419,7 +431,7 @@
             pltpu.SemaphoreType.DMA((6,)),
             pltpu.SemaphoreType.DMA((6,)),
             pltpu.SemaphoreType.DMA((6,)),
-            pltpu.SemaphoreType.DMA((2, RING)),
+            pltpu.SemaphoreType.DMA((RING,)),
             pltpu.SemaphoreType.DMA((2,)),
             pltpu.SemaphoreType.DMA((3,)),
         ],

time: 44 us -> 43.9 us (level)
  no operation moved by 1% of the time
where the time goes in v9:
time: 43.9 us; the launch traced here: 43.7 us
  Pallas kernels  43.1 us (98%)
  between operations  0.64 us (1%)
    pallas_call x1, Pallas kernels, shards(): pl.pallas_call(kernel, out_shape=shapes, in_specs=[hbm] * 4, out_specs=(v...  41.9 us
    pallas_call x1, Pallas kernels, shards(): pl.pallas_call(write, out_shape=shapes, in_specs=[vmem, vmem], out_specs=...  1.16 us

profile of v9, /device:TPU:1, one launch (start us, length us, event | category | flops | bytes accessed | tf_op | source)
XLA Modules:
  0.0 43.7 jit_solution(12825029390251204656)
XLA Ops:
  0.6 41.9 %quantizer_backward.1 = (f32[1024,256]{1,0:T(8,128)S(1)}, f32[512,256]{1,0:T(8,128)S(1)}) custom-call(bf16[1024,256]{1,0:T(8,128)(2,1)} %tok_hbm.1, bf16[1024,256]{1,0:T(8,128)(2,1)} %cot_hbm.1, bf16[2048,256]{1,0:T(8,128)(2,1)} %cb_hbm.1, s32[1,1024]{1,0:T(1,128)} %bitcast.1), custom_call_target="tpu_custom_call" | custom-call | tf_op jit(solution)/shard_map/quantizer_backward/pallas_call | solution.py:399
  42.6 1.2 %write_out.1 = (f32[1024,256]{1,0:T(8,128)}, f32[512,256]{1,0:T(8,128)}) custom-call(f32[1024,256]{1,0:T(8,128)S(1)} %get-tuple-element.4.grad_tok_ref, f32[512,256]{1,0:T(8,128)S(1)} %get-tuple-element.5.grad_cb_ref), custom_call_target="tpu_custom_call" | custom-call | tf_op jit(solution)/shard_map/write_out/pallas_call | solution.py:443

commit v10 on v9

--- a/solution.py
+++ b/solution.py
@@ -58,7 +58,6 @@
     back,
     direct,
     cbt,
-    v_first,
     uv_own,
     uv_other,
     uv_send,
@@ -185,7 +184,6 @@
         weight = expo[:, half * HALF : (half + 1) * HALF].astype(BF16)
         return jnp.dot(cbt[...], weight, preferred_element_type=F32)
 
-    v_first[...] = v_terms(0)
     stat_copy.wait()
 
     scale, mean = [], []
@@ -222,7 +220,7 @@
             uv_send[which, half, k] = both[k * ROWS : (k + 1) * ROWS].astype(BF16)
         uv_recv[which, half, first[half][1]] = uv_send[which, half, first[half][1]]
 
-    uv_chip(1, 0, v_first[...] * scale[0])
+    uv_chip(1, 0, v_terms(0) * scale[0])
     uv_chip(1, 1, v_terms(1) * scale[1])
     uv_chip(0, 0, u_terms(0))
     uv_chip(0, 1, u_terms(1))
@@ -411,7 +409,6 @@
             pltpu.VMEM((CODES, TOK), F32),
             pltpu.VMEM((CODES, D), F32),
             pltpu.VMEM((D, CODES), BF16),
-            pltpu.VMEM((D, HALF), F32),
             pltpu.VMEM((2, 2, 2, 128, HALF), BF16),
             pltpu.VMEM((2, 2, 128, HALF), BF16),
             pltpu.VMEM((2, 2, RING, ROWS, HALF), BF16),

time: 43.9 us -> 44.6 us (1.016)
  Pallas kernels: 43.1 us -> 43.9 us
    pallas_call x1, Pallas kernels: 41.9 us -> 42.7 us  [shards(): pl.pallas_call(kernel, out_shape=shapes, in_specs=[hbm] * 4, out_specs=(v...]
where the time goes in v10:
time: 44.6 us; the launch traced here: 44.5 us
  Pallas kernels  43.9 us (98%)
  between operations  0.64 us (1%)
    pallas_call x1, Pallas kernels, shards(): pl.pallas_call(kernel, out_shape=shapes, in_specs=[hbm] * 4, out_specs=(v...  42.7 us
    pallas_call x1, Pallas kernels, shards(): pl.pallas_call(write, out_shape=shapes, in_specs=[vmem, vmem], out_specs=...  1.16 us

profile of v10, /device:TPU:1, one launch (start us, length us, event | category | flops | bytes accessed | tf_op | source)
XLA Modules:
  0.0 44.5 jit_solution(11493200870152982446)
XLA Ops:
  0.6 42.7 %quantizer_backward.1 = (f32[1024,256]{1,0:T(8,128)S(1)}, f32[512,256]{1,0:T(8,128)S(1)}) custom-call(bf16[1024,256]{1,0:T(8,128)(2,1)} %tok_hbm.1, bf16[1024,256]{1,0:T(8,128)(2,1)} %cot_hbm.1, bf16[2048,256]{1,0:T(8,128)(2,1)} %cb_hbm.1, s32[1,1024]{1,0:T(1,128)} %bitcast.1), custom_call_target="tpu_custom_call" | custom-call | tf_op jit(solution)/shard_map/quantizer_backward/pallas_call | solution.py:397
  43.3 1.2 %write_out.1 = (f32[1024,256]{1,0:T(8,128)}, f32[512,256]{1,0:T(8,128)}) custom-call(f32[1024,256]{1,0:T(8,128)S(1)} %get-tuple-element.4.grad_tok_ref, f32[512,256]{1,0:T(8,128)S(1)} %get-tuple-element.5.grad_cb_ref), custom_call_target="tpu_custom_call" | custom-call | tf_op jit(solution)/shard_map/write_out/pallas_call | solution.py:440
